TPU v7x, 512 devices: a whole 4x4x16 slice. The times are simulated.
512 devices in a mesh: shard: 128 (over z, x, core), split: 4 (over y).
Axes of the slice: x: 4, y: 4, z: 16, core: 2. Of those that a mesh axis runs over, the one named last changes fastest.
Arguments:
- embeddings: bfloat16 [65536, 768], P(('shard', 'split')), may hold values from -160 to 160
- labels: int32 [65536], P(('shard', 'split')), may hold values from 0 to 1023, as said below
Outputs:
- weight: float32 [65536], P(('shard', 'split'))
Inputs may be any that keep to these rules, and one draw needn't show every extreme that they name: `labels`: cluster c belongs to owner c integer-divided by 8. On each device, the rows name the clusters of any one owner at most 4 times; on every device some owner is named exactly 4 times, and one owner is named 4 times on every device.
All inputs are finite; a program needn't handle non-finite values.
Results may differ from a plain program's by a relative error of at most 0.00041.
Values may be sent and summed in bfloat16 or wider, within the bound.
A program may use at most 64 MiB of HBM per device.

v0:
```python
import math

import jax
import jax.numpy as jnp
from jax import lax
from jax.sharding import PartitionSpec as P

CL_OWN = 8


inverse_temp = 10.0


def tile_sums(left, left_lab, right, right_lab):
    width = right.shape[0]
    tile = math.gcd(512, width)
    right_tiles = right.reshape(width // tile, tile, right.shape[1])
    lab_tiles = right_lab.reshape(width // tile, tile)

    def step(row_total, pair):
        block, block_lab = pair
        sims = lax.dot_general(
            left, block, (((1,), (1,)), ((), ())), preferred_element_type=jnp.float32
        )
        same = (left_lab[:, None] == block_lab[None, :]) & (block_lab[None, :] > 0)
        terms = jnp.where(same, jnp.exp(inverse_temp * sims), jnp.float32(0.0))
        return (row_total + jnp.sum(terms, axis=1), jnp.sum(terms, axis=0))

    start_total = jnp.zeros((left.shape[0],), jnp.float32)
    row_total, column_parts = lax.scan(step, start_total, (right_tiles, lab_tiles))
    return (row_total, column_parts.reshape(width))


def per_device(embeddings, labels):
    rows_dev = embeddings.shape[0]
    peers = lax.axis_size("shard")
    capacity = 4 * rows_dev // peers
    slots = peers * capacity
    wide = embeddings.astype(jnp.float32)
    norm_sq = jnp.sum(wide * wide, axis=1, keepdims=True) + 1e-06
    unit = (wide * lax.rsqrt(norm_sq)).astype(jnp.bfloat16)
    owner = labels // CL_OWN
    position = jnp.arange(rows_dev, dtype=jnp.int32)
    earlier = (owner[None, :] == owner[:, None]) & (position[None, :] < position[:, None])
    rank = jnp.sum(earlier.astype(jnp.int32), axis=1)
    slot_of_row = owner * capacity + rank
    placing = slot_of_row[None, :] == jnp.arange(slots, dtype=jnp.int32)[:, None]
    packed = jnp.dot(placing.astype(jnp.bfloat16), unit, preferred_element_type=jnp.float32).astype(
        jnp.bfloat16
    )
    packed_lab = jnp.sum(jnp.where(placing, labels[None, :] + 1, 0), axis=1)
    arrived, arrived_lab = (
        lax.all_to_all(
            packed.reshape(peers, capacity, -1), "shard", split_axis=0, concat_axis=0, tiled=True
        ),
        lax.all_to_all(
            packed_lab.reshape(peers, capacity), "shard", split_axis=0, concat_axis=0, tiled=True
        ),
    )
    mine = arrived.reshape(slots, -1)
    mine_lab = arrived_lab.reshape(slots)
    totals = tile_sums(
        mine,
        mine_lab,
        lax.all_gather(mine, "split", axis=0, tiled=True),
        lax.all_gather(mine_lab, "split", axis=0, tiled=True),
    )[0]
    weights_here = 0.1 * jnp.log(jnp.where(mine_lab > 0, totals, jnp.float32(1.0)))
    returned = lax.all_to_all(
        weights_here.reshape(peers, capacity), "shard", split_axis=0, concat_axis=0, tiled=True
    )
    return jnp.take(returned.reshape(slots), slot_of_row)


def solution(mesh):
    placed = (P(("shard", "split"), None), P(("shard", "split")))
    return jax.shard_map(
        per_device, mesh=mesh, in_specs=placed, out_specs=P(("shard", "split")), check_vma=False
    )
```

profile of v0, /device:TPU:1, one launch (start us, length us, event | category | flops | bytes accessed | tf_op | source)
XLA Modules:
  0.0 165.7 jit_solution(3787979542081002052)
XLA Ops:
  6.5 0.0 all-gather.3.cloned.1.call-start
  6.5 0.7 and_select_fusion.1
  7.2 0.2 convert_reduce_fusion
  7.4 1.1 fusion.7
  8.4 1.4 convolution_convert_fusion
  9.8 0.2 reshape.47
  10.0 61.6 %all_to_all.26 = bf16[128,4,768]{2,1,0:T(4,128)(2,1)S(1)} all-to-all(bf16[128,4,768]{2,1,0:T(4,128)(2,1)S(1)} %reshape.47), channel_id=1, replica_groups=mesh['shard'=128,'split'=4] {'shard'}, dimensions={0} | all-to-all | bytes 1572864 | tf_op jit(solution)/shard_map/all_to_all | solution.py:53
  71.6 1.1 reshape.48
  72.7 0.0 all-gather.3.cloned.1.call-update
  72.7 0.1 select_reduce_fusion
  72.8 0.7 all_to_all.17
  73.6 9.5 %all-to-all-start = ((s32[128,1,4]{2,1,0:T(1,128)}), s32[128,1,4]{2,1,0:T(1,128)S(1)}, u32[]{:S(2)}, u32[]{:S(2)}) async-start(s32[128,1,4]{2,1,0:T(1,128)} %bitcast), calls=%async_computation | async-start | bytes 131072 | tf_op jit(solution)/shard_map/all_to_all | solution.py:56
  83.1 14.9 %all-to-all-done = s32[128,1,4]{2,1,0:T(1,128)S(1)} async-done(((s32[128,1,4]{2,1,0:T(1,128)}), s32[128,1,4]{2,1,0:T(1,128)S(1)}, u32[]{:S(2)}, u32[]{:S(2)}) %all-to-all-start) | async-done | bytes 2080 | tf_op jit(solution)/shard_map/all_to_all | solution.py:56
  98.0 0.0 copy-start
  98.0 0.1 eq.73
  98.1 0.5 broadcast.62
  98.6 0.7 reduce.10
  99.3 0.1 reshape.60
  99.5 9.7 %all-gather = s32[4,1,512]{2,1,0:T(1,128)S(1)} all-gather(s32[1,1,512]{2,1,0:T(1,128)S(1)} %reshape.60), channel_id=1, replica_groups=mesh['shard'=128,'split'=4] {'split'}, dimensions={0}, use_global_device_ids=true | all-gather | bytes 10240 | tf_op jit(solution)/shard_map/all_gather | solution.py:66
  109.1 0.2 compare_reduce_fusion.1
  109.3 0.1 reshape.65
  109.4 5.2 %all-gather.3.cloned.1.call-done = bf16[2048,768]{1,0:T(8,128)(2,1)} async-done(((bf16[512,768]{1,0:T(8,128)(2,1)}), bf16[2048,768]{1,0:T(8,128)(2,1)}) %all-gather.3.cloned.1.call-update) | async-done | bytes 3145744 | tf_op jit(solution)/shard_map/all_gather | solution.py:65
  114.6 0.0 copy-done
  114.6 8.8 %while.12 = (s32[]{:T(128)}, f32[512]{0:T(512)S(1)}, s32[128,4]{1,0:T(8,128)}, s32[4,512]{1,0:T(4,128)S(1)}, bf16[4,512,768]{2,1,0:T(8,128)(2,1)}, /*index=5*/bf...) while((s32[]{:T(128)}, f32[512]{0:T(512)S(1)}, s32[128,4]{1,0:T(8,128)}, ...), condition=%wide.wide.region_5.6_spmd.clone, body=%wide.wide.region_3.5_spmd.clone.sunk | while | flops 403964928 | bytes 1590891 | solution.py:30
  114.7 2.1 %fusion.22 = f32[512]{0:T(512)S(1)} fusion(bf16[512,768]{1,0:T(8,128)(2,1)} %get-tuple-element.173, bf16[4,512,768]{2,1,0:T(8,128)(2,1)} %get-tuple-element.172, s32[]{:T(128)} %get-tuple-element.159, s32[512]{0:T(512)S(1)} %get-tuple-element.174, s32[512]{0:T(512)S(1)} %bitcast.32, pred[512]{0:T(512)(128)(4,1)S(1)} %get-tuple-element.149), kind=kOutput, calls=%fused_computation.5.clone.clone.1 | convolution fusion | flops 403963392 | bytes 1580032 | tf_op jit(solution)/shard_map/while/body/eval_jaxpr/dot_general | solution.py:22
  116.9 2.1 %fusion.22 = f32[512]{0:T(512)S(1)} fusion(bf16[512,768]{1,0:T(8,128)(2,1)} %get-tuple-element.173, bf16[4,512,768]{2,1,0:T(8,128)(2,1)} %get-tuple-element.172, s32[]{:T(128)} %get-tuple-element.159, s32[512]{0:T(512)S(1)} %get-tuple-element.174, s32[512]{0:T(512)S(1)} %bitcast.32, pred[512]{0:T(512)(128)(4,1)S(1)} %get-tuple-element.149), kind=kOutput, calls=%fused_computation.5.clone.clone.1 | convolution fusion | flops 403963392 | bytes 1580032 | tf_op jit(solution)/shard_map/while/body/eval_jaxpr/dot_general | solution.py:22
  119.1 2.1 %fusion.22 = f32[512]{0:T(512)S(1)} fusion(bf16[512,768]{1,0:T(8,128)(2,1)} %get-tuple-element.173, bf16[4,512,768]{2,1,0:T(8,128)(2,1)} %get-tuple-element.172, s32[]{:T(128)} %get-tuple-element.159, s32[512]{0:T(512)S(1)} %get-tuple-element.174, s32[512]{0:T(512)S(1)} %bitcast.32, pred[512]{0:T(512)(128)(4,1)S(1)} %get-tuple-element.149), kind=kOutput, calls=%fused_computation.5.clone.clone.1 | convolution fusion | flops 403963392 | bytes 1580032 | tf_op jit(solution)/shard_map/while/body/eval_jaxpr/dot_general | solution.py:22
  121.3 2.1 %fusion.22 = f32[512]{0:T(512)S(1)} fusion(bf16[512,768]{1,0:T(8,128)(2,1)} %get-tuple-element.173, bf16[4,512,768]{2,1,0:T(8,128)(2,1)} %get-tuple-element.172, s32[]{:T(128)} %get-tuple-element.159, s32[512]{0:T(512)S(1)} %get-tuple-element.174, s32[512]{0:T(512)S(1)} %bitcast.32, pred[512]{0:T(512)(128)(4,1)S(1)} %get-tuple-element.149), kind=kOutput, calls=%fused_computation.5.clone.clone.1 | convolution fusion | flops 403963392 | bytes 1580032 | tf_op jit(solution)/shard_map/while/body/eval_jaxpr/dot_general | solution.py:22
  123.4 0.7 all_to_all.21
  124.2 16.6 %all-to-all-start.2 = ((f32[128,1,4]{2,1,0:T(1,128)}), f32[128,1,4]{2,1,0:T(1,128)S(1)}, u32[]{:S(2)}, u32[]{:S(2)}) async-start(f32[128,1,4]{2,1,0:T(1,128)} %bitcast.3), calls=%async_computation.2 | async-start | bytes 131072 | tf_op jit(solution)/shard_map/all_to_all | solution.py:69
  140.8 14.8 %all-to-all-done.2 = f32[128,1,4]{2,1,0:T(1,128)S(1)} async-done(((f32[128,1,4]{2,1,0:T(1,128)}), f32[128,1,4]{2,1,0:T(1,128)S(1)}, u32[]{:S(2)}, u32[]{:S(2)}) %all-to-all-start.2) | async-done | bytes 2080 | tf_op jit(solution)/shard_map/all_to_all | solution.py:69
  155.6 0.5 broadcast.63
  156.1 0.8 reduce.11
  157.0 0.1 reshape.50
  157.1 1.3 gather_fusion
  158.3 0.5 and_select_fusion
  (14 shorter events, 0.2 us)
Async XLA Ops:
  6.5 108.1 %all-gather.3.cloned.1.call-start = ((), (), s32[]{:S(2)}) async-start(), calls=%async_computation.3 | async-start | bytes 3932160 | tf_op jit(solution)/shard_map/all_gather | solution.py:65
  73.6 24.4 %all-to-all-start = ((s32[128,1,4]{2,1,0:T(1,128)}), s32[128,1,4]{2,1,0:T(1,128)S(1)}, u32[]{:S(2)}, u32[]{:S(2)}) async-start(s32[128,1,4]{2,1,0:T(1,128)} %bitcast), calls=%async_computation | async-start | bytes 131072 | tf_op jit(solution)/shard_map/all_to_all | solution.py:56
  98.0 16.6 %copy-start = (s32[128,1,4]{2,1,0:T(1,128)}, s32[128,1,4]{2,1,0:T(1,128)S(1)}, u32[]{:S(2)}) copy-start(s32[128,1,4]{2,1,0:T(1,128)S(1)} %all-to-all-done) | copy-start | bytes 6148
  124.2 31.5 %all-to-all-start.2 = ((f32[128,1,4]{2,1,0:T(1,128)}), f32[128,1,4]{2,1,0:T(1,128)S(1)}, u32[]{:S(2)}, u32[]{:S(2)}) async-start(f32[128,1,4]{2,1,0:T(1,128)} %bitcast.3), calls=%async_computation.2 | async-start | bytes 131072 | tf_op jit(solution)/shard_map/all_to_all | solution.py:69
Sparse Core Ops, SparseCore 0:
  72.8 41.7 all-gather.2
where the time goes:
time: 166 us
  blocking collectives  71.3 us (43%)
  waiting for transfers between devices  35 us (21%)
  starting transfers between devices  26.1 us (16%)
  between operations  13.5 us (8%)
  matrix products  9.89 us (6%)
  local copies, waits for them, and re-layouts  5.43 us (3%)
  other arithmetic  4.47 us (3%)
    all_to_all x1, blocking collectives, per_device(): lax.all_to_all(packed.reshape(peers, capacity, -1), 'shard', split_axis=0...  61.6 us
    all_to_all x1, starting transfers between devices, per_device(): lax.all_to_all(weights_here.reshape(peers, capacity), 'shard', split_axis...  16.6 us
    all_to_all x1, waiting for transfers between devices, per_device(): lax.all_to_all(packed_lab.reshape(peers, capacity), 'shard', split_axis=0...  14.9 us
    all_to_all x1, waiting for transfers between devices, per_device(): lax.all_to_all(weights_here.reshape(peers, capacity), 'shard', split_axis...  14.8 us
    all_gather x1, blocking collectives, per_device(): lax.all_gather(mine_lab, 'split', axis=0, tiled=True)  9.66 us
    all_to_all x1, starting transfers between devices, per_device(): lax.all_to_all(packed_lab.reshape(peers, capacity), 'shard', split_axis=0...  9.49 us
    dot_general x4, matrix products, step(): lax.dot_general(left, block, (((1,), (1,)), ((), ())), preferred_element_...  8.53 us
    all_gather x1, waiting for transfers between devices, per_device(): lax.all_gather(mine, 'split', axis=0, tiled=True)  5.2 us
  transfers between devices with their start and end apart: 3, of which 3 were waited for; matrix products, arithmetic and copies ran while one was open for 1% of the time, Pallas kernels for 0%

commit v1 on v0

v1 whole, which is shorter than its diff:
```python
import functools

import jax
import jax.numpy as jnp
from jax import lax
from jax.experimental import pallas as pl
from jax.experimental.pallas import tpu as pltpu
from jax.sharding import PartitionSpec as P

MESH = pl.DeviceIdType.MESH
F32 = jnp.float32
BF16 = jnp.bfloat16

D = 768
EXT = 128
WIDE = D + EXT
ROWS = 128
NZ, NX, NY = 16, 4, 4
PIECE = 64
PENALTY = 16.0
LOG2E10 = 14.426950408889634


def one_hot(cond):
    return jnp.where(cond, 1.0, 0.0).astype(BF16)


def dot_nn(a, b):
    return lax.dot_general(a, b, (((1,), (0,)), ((), ())), preferred_element_type=F32)


def dot_nt(a, b):
    return lax.dot_general(a, b, (((1,), (1,)), ((), ())), preferred_element_type=F32)


def iota(shape, dim):
    return lax.broadcasted_iota(jnp.int32, shape, dim)


def kernel(
    emb_ref, lab_ref, out_ref,
    unit, raw, fsend, farr, meta, psend, own, sib, left, acc, colacc, tot, back, ret, wts,
    raw_send, raw_recv, far_send, far_recv, meta_send, meta_recv, plane_send, own_recv,
    sib_send, sib_recv, tot_send, tot_recv, ret_send, ret_recv,
):
    p = lax.axis_index("shard")
    y = lax.axis_index("split")
    z = p // 8
    x = (p % 8) // 2
    c = p % 2
    xy = x * NY + y
    turn = (y - x + NY) % NY
    handles = turn % 2 == 0
    my_owner = x * 2 + turn // 2

    def at(zz, xx, cc, yy):
        return (zz * 8 + xx * 2 + cc, yy)

    def handler_y(j):
        return (2 * (j % 2) + j // 2) % NY

    def up(pos):
        k = (pos + 1) // 2
        return (z + jnp.where(pos % 2 == 1, k, NZ - k)) % NZ

    def down(pos):
        k = (pos + 1) // 2
        return (z + jnp.where(pos % 2 == 1, NZ - k, k)) % NZ

    barrier = pltpu.get_barrier_semaphore()

    def greet(device):
        pl.semaphore_signal(barrier, inc=1, device_id=device, device_id_type=MESH)

    def greet_z(i, _):
        greet(at((z + i) % NZ, x, c, y))
        return 0

    lax.fori_loop(1, NZ, greet_z, 0)
    greet(at(z, x, 1 - c, y))

    def greet_handler(j, _):
        @pl.when(jnp.logical_or(j // 2 != x, handler_y(j) != y))
        def _():
            greet(at(z, j // 2, c, handler_y(j)))
        return 0

    lax.fori_loop(0, 8, greet_handler, 0)

    @pl.when(handles)
    def _():
        def greet_relay(i, _):
            @pl.when(i != xy)
            def _():
                greet(at(z, i // NY, c, i % NY))
            return 0

        lax.fori_loop(0, NX * NY, greet_relay, 0)

    wide = emb_ref[...].astype(F32)
    norm_sq = jnp.sum(wide * wide, axis=1, keepdims=True) + 1e-06
    unit[...] = (wide * lax.rsqrt(norm_sq)).astype(BF16)
    label = lab_ref[...]
    owner = label >> 3
    owner_f = jnp.broadcast_to(owner.astype(F32), (ROWS, ROWS))
    earlier = (owner_f == owner_f.T) & (iota((ROWS, ROWS), 0) < iota((ROWS, ROWS), 1))
    rank = jnp.sum(jnp.where(earlier, 1.0, 0.0), axis=0, keepdims=True).astype(jnp.int32)
    meta[0] = label * 4 + rank

    pl.semaphore_wait(barrier, jnp.where(handles, 38, 24))

    def raw_copy(way, hop, piece):
        rows = pl.ds(piece * PIECE, PIECE)
        src = unit.at[rows] if hop == 0 else raw.at[way, 0, rows]
        to = (z + (1 if way == 0 else NZ - 1)) % NZ
        return pltpu.make_async_remote_copy(
            src_ref=src, dst_ref=raw.at[way, hop, rows],
            send_sem=raw_send.at[way, hop, piece], recv_sem=raw_recv.at[way, hop, piece],
            device_id=at(to, x, c, y), device_id_type=MESH,
        )

    pieces = ROWS // PIECE
    for piece in range(pieces):
        for way in range(2):
            raw_copy(way, 0, piece).start()

    def meta_copy(pos):
        return pltpu.make_async_remote_copy(
            src_ref=meta.at[0], dst_ref=meta.at[pos],
            send_sem=meta_send.at[pos], recv_sem=meta_recv,
            device_id=at(up(pos), x, c, y), device_id_type=MESH,
        )

    def meta_start(pos, _):
        meta_copy(pos).start()
        return 0

    lax.fori_loop(1, NZ, meta_start, 0)

    def slots_of(code):
        return ((code >> 5) << 2) | (code & 3)

    def pack_near(pos, rows_ref):
        slot = slots_of(meta[pos])
        pick = one_hot(slot == z * 32 + iota((32, ROWS), 0))
        farr[pl.ds(pos * 32, 32), :] = dot_nn(pick, rows_ref[...]).astype(BF16)

    pack_near(0, unit)

    for piece in range(pieces):
        for way in range(2):
            raw_copy(way, 0, piece).wait_recv()
            raw_copy(way, 1, piece).start()

    pltpu.make_async_copy(meta.at[pl.ds(1, NZ - 1)], meta.at[pl.ds(1, NZ - 1)], meta_recv).wait()
    pack_near(1, raw.at[0, 0])
    pack_near(2, raw.at[1, 0])

    def far_copy(way, g):
        to = (z + (1 + g if way == 0 else NZ - 1 - g)) % NZ
        if g < 5:
            pos = 2 * g + 5 + way
            src, dst, sem = fsend.at[way, pl.ds(g * 32, 32)], farr.at[pl.ds(pos * 32, 32)], pos
        else:
            src = fsend.at[way, pl.ds(160 + way * 16, 16)]
            dst, sem = farr.at[pl.ds(480 + way * 16, 16)], 15 + way
        return pltpu.make_async_remote_copy(
            src_ref=src, dst_ref=dst, send_sem=far_send.at[way, g], recv_sem=far_recv.at[sem],
            device_id=at(to, x, c, y), device_id_type=MESH,
        )

    for way in range(2):
        for piece in range(pieces):
            raw_copy(way, 1, piece).wait_recv()
        slot = slots_of(meta[3 + way])
        row = iota((192, ROWS), 0)
        step = 1 + (row >> 5)
        plane = (z + (step if way == 0 else NZ - step)) & (NZ - 1)
        pick = one_hot(slot == (plane << 5) + (row & 31))
        fsend[way] = dot_nn(pick, raw[way, 1]).astype(BF16)
        for g in range(6):
            far_copy(way, g).start()

    pack_near(3, raw.at[0, 1])
    pack_near(4, raw.at[1, 1])

    def plane_dst(q):
        return own.at[pl.ds(q * 256 + pl.multiple_of(xy * 16, 16), 16)]

    def plane_copy(q, j):
        return pltpu.make_async_remote_copy(
            src_ref=psend.at[pl.ds(q * ROWS + pl.multiple_of(j * 16, 16), 16)], dst_ref=plane_dst(q),
            send_sem=plane_send.at[q, j], recv_sem=own_recv.at[q],
            device_id=at(z, j // 2, c, handler_y(j)), device_id_type=MESH,
        )

    def relay(q):
        here = pl.ds(q * ROWS, ROWS)
        i = iota((ROWS, ROWS), 0)
        lane = iota((ROWS, ROWS), 1)
        zq, j4 = (i >> 2) & 3, ((i >> 4) << 2) | (i & 3)
        order = one_hot(lane == zq * 32 + j4)
        psend[here, :D] = dot_nn(order, farr[here, :]).astype(BF16)
        same = jnp.zeros((ROWS, EXT), F32)
        for k in range(4):
            code = meta[q * 4 + k]
            pick = one_hot((slots_of(code) == z * 32 + j4) & (zq == k))
            same += dot_nt(pick, one_hot((((code >> 2) & 7) == i) | (i == 8)))
        right = jnp.where(lane < 8, PENALTY * same - PENALTY, jnp.where(lane == 8, -PENALTY * same, 0.0))
        psend[here, D:] = right.astype(BF16)

        def send(j, _):
            mine = jnp.logical_and(j // 2 == x, handler_y(j) == y)

            @pl.when(mine)
            def _():
                pltpu.make_async_copy(
                    psend.at[pl.ds(q * ROWS + pl.multiple_of(j * 16, 16), 16)], plane_dst(q), own_recv.at[q]
                ).start()

            @pl.when(jnp.logical_not(mine))
            def _():
                plane_copy(q, j).start()
            return 0

        lax.fori_loop(0, 8, send, 0)

    def sib_copy(q):
        rows = pl.ds(q * 256, 256)
        return pltpu.make_async_remote_copy(
            src_ref=own.at[rows], dst_ref=sib.at[rows], send_sem=sib_send.at[q], recv_sem=sib_recv.at[q],
            device_id=at(z, x, 1 - c, y), device_id_type=MESH,
        )

    def terms(a, right_ref, b):
        sims = dot_nt(left[pl.ds(a * 256, 256), :], right_ref[pl.ds(b * 256, 256), :])
        return jnp.exp2(sims * LOG2E10)

    def add_rows(a, e):
        rows = pl.ds(a * 256, 256)
        acc[rows, :] = acc[rows, :] + (e[:, :128] + e[:, 128:])

    def handle(q):
        @pl.when(handles)
        def _():
            rows = pl.ds(q * 256, 256)
            pltpu.make_async_copy(own.at[rows], own.at[rows], own_recv.at[q]).wait()
            sib_copy(q).start()
            left[rows, :D] = own[rows, :D]
            is_cluster = iota((256, EXT), 1) < 9
            left[rows, D:] = jnp.where(
                is_cluster, own[rows, D:].astype(F32) * (1.0 / PENALTY) + 1.0, 0.0
            ).astype(BF16)
            e = terms(q, own, q)
            acc[rows, :] = e[:, :128] + e[:, 128:]
            colacc[q] = jnp.zeros((8, 256), F32)

            def own_pair(a, _):
                e = terms(a, own, q)
                add_rows(a, e)
                colacc[q] = colacc[q] + jnp.sum(e.reshape(32, 8, 256), axis=0)
                return 0

            lax.fori_loop(0, q, own_pair, 0)
            sib_copy(q).wait_recv()

            def sib_new(a, _):
                add_rows(a, terms(a, sib, q))
                return 0

            lax.fori_loop(0, q + 1, sib_new, 0)

            def sib_old(b, _):
                add_rows(q, terms(q, sib, b))
                return 0

            lax.fori_loop(0, q, sib_old, 0)

    relay(0)
    for pos in (5, 6, 7):
        far_copy((pos - 5) % 2, (pos - 5) // 2).wait_recv()
    relay(1)
    handle(0)
    handle(1)
    for pos in (8, 9, 10, 11):
        far_copy((pos - 5) % 2, (pos - 5) // 2).wait_recv()
    relay(2)
    handle(2)
    for pos in (12, 13, 14):
        far_copy((pos - 5) % 2, (pos - 5) // 2).wait_recv()
    far_copy(0, 5).wait_recv()
    far_copy(1, 5).wait_recv()
    relay(3)
    handle(3)

    def tot_copy(i):
        return pltpu.make_async_remote_copy(
            src_ref=tot.at[i // 8], dst_ref=back.at[my_owner],
            send_sem=tot_send.at[i], recv_sem=tot_recv,
            device_id=at(z, i // NY, c, i % NY), device_id_type=MESH,
        )

    @pl.when(handles)
    def _():
        for q in range(4):
            for h in range(2):
                part = acc[pl.ds(q * 256 + h * 128, 128), :].T
                total = jnp.sum(part, axis=0, keepdims=True) + jnp.sum(
                    colacc[q, :, h * 128 : h * 128 + 128], axis=0, keepdims=True
                )
                tot[h, q : q + 1, :] = total
        tot[0, 4:8, :] = jnp.zeros((4, 128), F32)
        tot[1, 4:8, :] = jnp.zeros((4, 128), F32)

        def send(i, _):
            @pl.when(i == xy)
            def _():
                pltpu.make_async_copy(tot.at[i // 8], back.at[my_owner], tot_recv).start()

            @pl.when(i != xy)
            def _():
                tot_copy(i).start()
            return 0

        lax.fori_loop(0, NX * NY, send, 0)

    pltpu.make_async_copy(back, back, tot_recv).wait()
    for j in range(8):
        for q in range(4):
            ret[q, j : j + 1, :] = back[j, q : q + 1, :]

    def ret_copy(pos):
        return pltpu.make_async_remote_copy(
            src_ref=ret.at[pos // 4], dst_ref=wts.at[z],
            send_sem=ret_send.at[pos], recv_sem=ret_recv,
            device_id=at(down(pos), x, c, y), device_id_type=MESH,
        )

    def ret_start(pos, _):
        ret_copy(pos).start()
        return 0

    lax.fori_loop(1, NZ, ret_start, 0)
    wts[z] = ret[0]
    pltpu.make_async_copy(
        wts.at[pl.ds(0, NZ - 1)], wts.at[pl.ds(0, NZ - 1)], ret_recv
    ).wait()

    code = meta[0]
    table = wts[...].reshape(NZ * 8, 128).T
    lines = jnp.where((code >> 5) == iota((NZ * 8, ROWS), 0), 1.0, 0.0)
    picked = jnp.dot(table, lines, precision=lax.Precision.HIGHEST, preferred_element_type=F32)
    ahead = ((code >> 8) - z) & (NZ - 1)
    pos = jnp.where(ahead == 0, 0, jnp.where(ahead <= 8, 2 * ahead - 1, 2 * (NZ - ahead)))
    lane = (xy % 8) * 16 + (pos & 3) * 4 + (code & 3)
    total = jnp.sum(jnp.where(iota((128, ROWS), 0) == lane, picked, 0.0), axis=0, keepdims=True)
    out_ref[...] = 0.1 * jnp.log(total)

    for way in range(2):
        for hop in range(2):
            for piece in range(pieces):
                raw_copy(way, hop, piece).wait_send()
        for g in range(6):
            far_copy(way, g).wait_send()

    def drain_z(pos, _):
        meta_copy(pos).wait_send()
        ret_copy(pos).wait_send()
        return 0

    lax.fori_loop(1, NZ, drain_z, 0)

    def drain_plane(j, _):
        @pl.when(jnp.logical_or(j // 2 != x, handler_y(j) != y))
        def _():
            for q in range(4):
                plane_copy(q, j).wait_send()
        return 0

    lax.fori_loop(0, 8, drain_plane, 0)

    @pl.when(handles)
    def _():
        for q in range(4):
            sib_copy(q).wait_send()

        def drain_tot(i, _):
            @pl.when(i != xy)
            def _():
                tot_copy(i).wait_send()
            return 0

        lax.fori_loop(0, NX * NY, drain_tot, 0)


def per_device(embeddings, labels):
    dma = pltpu.SemaphoreType.DMA
    vmem = pltpu.VMEM
    weight = pl.pallas_call(
        kernel,
        out_shape=jax.ShapeDtypeStruct((1, ROWS), F32),
        in_specs=[pl.BlockSpec(memory_space=pltpu.VMEM)] * 2,
        out_specs=pl.BlockSpec(memory_space=pltpu.VMEM),
        scratch_shapes=[
            vmem((ROWS, D), BF16),
            vmem((2, 2, ROWS, D), BF16),
            vmem((2, 192, D), BF16),
            vmem((NZ * 32, D), BF16),
            vmem((NZ, 1, ROWS), jnp.int32),
            vmem((4 * ROWS, WIDE), BF16),
            vmem((1024, WIDE), BF16),
            vmem((1024, WIDE), BF16),
            vmem((1024, WIDE), BF16),
            vmem((1024, 128), F32),
            vmem((4, 8, 256), F32),
            vmem((2, 8, 128), F32),
            vmem((8, 8, 128), F32),
            vmem((4, 8, 128), F32),
            vmem((NZ, 8, 128), F32),
            dma((2, 2, ROWS // PIECE)), dma((2, 2, ROWS // PIECE)),
            dma((2, 6)), dma((17,)),
            dma((NZ,)), dma,
            dma((4, 8)), dma((4,)),
            dma((4,)), dma((4,)),
            dma((NX * NY,)), dma,
            dma((NZ,)), dma,
        ],
        compiler_params=pltpu.CompilerParams(
            collective_id=0, has_side_effects=True, vmem_limit_bytes=40 * 1024 * 1024
        ),
        name="soft_dedup",
    )(embeddings, labels.reshape(1, ROWS))
    return weight.reshape(ROWS)


def solution(mesh):
    placed = (P(("shard", "split"), None), P(("shard", "split")))
    return jax.shard_map(
        per_device, mesh=mesh, in_specs=placed, out_specs=P(("shard", "split")), check_vma=False
    )
```

time: 166 us -> 82.6 us (0.50)
  Pallas kernels: 0 us -> 80.3 us
  blocking collectives: 71.3 us -> 0 us
  waiting for transfers between devices: 35 us -> 0 us
  starting transfers between devices: 26.1 us -> 0 us
  between operations: 13.5 us -> 0.01 us
  matrix products: 9.89 us -> 0 us
  other arithmetic: 4.47 us -> 0 us
  local copies, waits for them, and re-layouts: 5.43 us -> 2.09 us
    pallas_call x0 -> x1, Pallas kernels: none -> 80.3 us  [per_device(): pl.pallas_call(kernel, out_shape=jax.ShapeDtypeStruct((1, ROWS), F32), in...]
    all_to_all x1 -> x0, blocking collectives: 61.6 us -> none  [per_device(): lax.all_to_all(packed.reshape(peers, capacity, -1), 'shard', split_axis=0...]
    all_to_all x2 -> x0, waiting for transfers between devices: 29.7 us -> none  [the longest x1 14.9 us: per_device(): lax.all_to_all(packed_lab.reshape(peers, capacity), 'shard', split_axis=0...]
    all_to_all x2 -> x0, starting transfers between devices: 26.1 us -> none  [the longest x1 16.6 us: per_device(): lax.all_to_all(weights_here.reshape(peers, capacity), 'shard', split_axis...]
    dot_general x5 -> x0, matrix products: 9.89 us -> none  [the longest x4 8.53 us: step(): lax.dot_general(left, block, (((1,), (1,)), ((), ())), preferred_element_...]
    all_gather x1 -> x0, blocking collectives: 9.66 us -> none  [per_device(): lax.all_gather(mine_lab, 'split', axis=0, tiled=True)]
    all_gather x1 -> x0, waiting for transfers between devices: 5.2 us -> none  [per_device(): lax.all_gather(mine, 'split', axis=0, tiled=True)]
    all_to_all x4 -> x0, local copies, waits for them, and re-layouts: 2.48 us -> none  [the longest x2 1.24 us: per_device(): lax.all_to_all(packed_lab.reshape(peers, capacity), 'shard', split_axis=0...]
  transfers between devices with their start and end apart: 3 -> 0, of which waited for: 3 -> 0; matrix products, arithmetic and copies ran while one was open for 1% -> 0% of each run, Pallas kernels for 0% -> 0%
where the time goes in v1:
time: 82.6 us; the launch traced here: 82.4 us
  Pallas kernels  80.3 us (97%)
  local copies, waits for them, and re-layouts  2.09 us (3%)
    pallas_call x1, Pallas kernels, per_device(): pl.pallas_call(kernel, out_shape=jax.ShapeDtypeStruct((1, ROWS), F32), in...  80.3 us
    unnamed x5, local copies, waits for them, and re-layouts  2.09 us

profile of v1, /device:TPU:1, one launch (start us, length us, event | category | flops | bytes accessed | tf_op | source)
XLA Modules:
  0.0 82.4 jit_solution(10670052595354730270)
XLA Ops:
  0.0 0.0 copy-start.1
  0.0 0.7 copy-done.1
  0.7 0.0 copy-start
  0.7 0.9 %copy-done = bf16[128,768]{1,0:T(8,128)(2,1)S(1)} copy-done((bf16[128,768]{1,0:T(8,128)(2,1)S(1)}, bf16[128,768]{1,0:T(8,128)(2,1)}, u32[]{:S(2)}) %copy-start) | copy-done | bytes 196632
  1.6 80.3 %soft_dedup.1 = f32[1,128]{1,0:T(1,128)S(1)} custom-call(bf16[128,768]{1,0:T(8,128)(2,1)S(1)} %copy-done, s32[1,128]{1,0:T(1,128)S(1)} %bitcast.2), custom_call_target="tpu_custom_call" | custom-call | tf_op jit(solution)/shard_map/soft_dedup/pallas_call | solution.py:399
  81.9 0.5 copy.4
Async XLA Ops:
  0.0 0.7 copy-start.1
  0.7 0.9 %copy-start = (bf16[128,768]{1,0:T(8,128)(2,1)S(1)}, bf16[128,768]{1,0:T(8,128)(2,1)}, u32[]{:S(2)}) copy-start(bf16[128,768]{1,0:T(8,128)(2,1)} %emb_ref.1) | copy-start | bytes 589828

commit v2 on v1

v2 whole, which is shorter than its diff:
```python
import functools

import jax
import jax.numpy as jnp
from jax import lax
from jax.experimental import pallas as pl
from jax.experimental.pallas import tpu as pltpu
from jax.sharding import PartitionSpec as P

MESH = pl.DeviceIdType.MESH
F32 = jnp.float32
BF16 = jnp.bfloat16

D = 768
EXT = 128
WIDE = D + EXT
ROWS = 128
NZ, NX, NY = 16, 4, 4
PIECE = 64
PENALTY = 16.0
LOG2E10 = 14.426950408889634


def one_hot(cond):
    return jnp.where(cond, 1.0, 0.0).astype(BF16)


def dot_nn(a, b):
    return lax.dot_general(a, b, (((1,), (0,)), ((), ())), preferred_element_type=F32)


def dot_nt(a, b):
    return lax.dot_general(a, b, (((1,), (1,)), ((), ())), preferred_element_type=F32)


def iota(shape, dim):
    return lax.broadcasted_iota(jnp.int32, shape, dim)


def kernel(
    emb_hbm, lab_hbm, out_ref,
    emb, lab, unit, raw, fsend, farr, meta, psend, pext, own, sib, left, acc, colacc, tot, back, ret, wts,
    in_sem, known, raw_send, raw_recv, far_send, far_recv, meta_send, meta_recv, plane_send, own_recv,
    ext_send, ext_recv, sib_send, sib_recv, tot_send, tot_recv, ret_send, ret_recv,
):
    p = lax.axis_index("shard")
    y = lax.axis_index("split")
    z = p // 8
    x = (p % 8) // 2
    c = p % 2
    xy = x * NY + y
    turn = (y - x + NY) % NY
    handles = turn % 2 == 0
    my_owner = x * 2 + turn // 2

    def at(zz, xx, cc, yy):
        return (zz * 8 + xx * 2 + cc, yy)

    def handler_y(j):
        return (2 * (j % 2) + j // 2) % NY

    def up(pos):
        k = (pos + 1) // 2
        return (z + jnp.where(pos % 2 == 1, k, NZ - k)) % NZ

    def down(pos):
        k = (pos + 1) // 2
        return (z + jnp.where(pos % 2 == 1, NZ - k, k)) % NZ

    barrier = pltpu.get_barrier_semaphore()
    z_by = lambda k: at((z + k + NZ) & (NZ - 1), x, c, y)
    x_by = lambda k: at(z, (x + k) & 3, c, y)
    y_by = lambda k: at(z, x, c, (y + k) & 3)
    near = [z_by(1), z_by(-1), x_by(1), x_by(3), y_by(1), y_by(3)]
    for device in near + [at(z, x, 1 - c, y)]:
        pl.semaphore_signal(barrier, inc=1, device_id=device, device_id_type=MESH)
    load_emb = pltpu.make_async_copy(emb_hbm, emb, in_sem.at[0])
    load_lab = pltpu.make_async_copy(lab_hbm, lab, in_sem.at[1])
    load_lab.start()
    load_emb.start()

    rounds = [
        near,
        [z_by(2), z_by(-2)],
        [z_by(4), z_by(-4)],
        [y_by(1), y_by(2), y_by(3)],
        [x_by(1), x_by(2), x_by(3)],
    ]

    def tell(r):
        for device in rounds[r]:
            pl.semaphore_signal(known.at[r], inc=1, device_id=device, device_id_type=MESH)

    def learn(r):
        pl.semaphore_wait(known.at[r], len(rounds[r]))

    load_lab.wait()
    load_emb.wait()
    wide = emb[...].astype(F32)
    norm_sq = jnp.sum(wide * wide, axis=1, keepdims=True) + 1e-06
    unit[...] = (wide * lax.rsqrt(norm_sq)).astype(BF16)
    label = lab[...]
    owner = label >> 3
    owner_f = jnp.broadcast_to(owner.astype(F32), (ROWS, ROWS))
    earlier = (owner_f == owner_f.T) & (iota((ROWS, ROWS), 0) < iota((ROWS, ROWS), 1))
    rank = jnp.sum(jnp.where(earlier, 1.0, 0.0), axis=0, keepdims=True).astype(jnp.int32)
    meta[0] = label * 4 + rank

    pl.semaphore_wait(barrier, 7)

    def raw_copy(way, hop, piece):
        rows = pl.ds(piece * PIECE, PIECE)
        src = unit.at[rows] if hop == 0 else raw.at[way, 0, rows]
        to = (z + (1 if way == 0 else NZ - 1)) % NZ
        return pltpu.make_async_remote_copy(
            src_ref=src, dst_ref=raw.at[way, hop, rows],
            send_sem=raw_send.at[way, hop, piece], recv_sem=raw_recv.at[way, hop, piece],
            device_id=at(to, x, c, y), device_id_type=MESH,
        )

    pieces = ROWS // PIECE
    for piece in range(pieces):
        for way in range(2):
            raw_copy(way, 0, piece).start()

    def meta_copy(pos, sem):
        return pltpu.make_async_remote_copy(
            src_ref=meta.at[0], dst_ref=meta.at[pos],
            send_sem=meta_send.at[pos], recv_sem=meta_recv.at[sem],
            device_id=at(up(pos), x, c, y), device_id_type=MESH,
        )

    meta_copy(1, 0).start()
    meta_copy(2, 0).start()
    tell(0)
    learn(0)
    meta_copy(3, 0).start()
    meta_copy(4, 0).start()
    tell(1)
    learn(1)
    tell(2)

    def slots_of(code):
        return ((code >> 5) << 2) | (code & 3)

    def pack_near(pos, rows_ref):
        slot = slots_of(meta[pos])
        pick = one_hot(slot == z * 32 + iota((32, ROWS), 0))
        farr[pl.ds(pos * 32, 32), :] = dot_nn(pick, rows_ref[...]).astype(BF16)

    def far_copy(way, g):
        step = 1 + g if g < 5 else 7
        to = (z + (step if way == 0 else NZ - step)) & (NZ - 1)
        if g < 5:
            pos = 2 * g + 5 + way
            src, dst, sem = fsend.at[way, pl.ds(g * 32, 32)], farr.at[pl.ds(pos * 32, 32)], pos
        else:
            src = fsend.at[way, pl.ds(160, 16)]
            dst, sem = farr.at[pl.ds(480 + way * 16, 16)], 15 + way
        return pltpu.make_async_remote_copy(
            src_ref=src, dst_ref=dst, send_sem=far_send.at[way, g], recv_sem=far_recv.at[sem],
            device_id=at(to, x, c, y), device_id_type=MESH,
        )

    for piece in range(pieces):
        for way in range(2):
            raw_copy(way, 0, piece).wait_recv()
            raw_copy(way, 1, piece).start()
        if piece == 0:
            learn(2)
            tell(3)
    near_meta = meta.at[pl.ds(1, 4)]
    pltpu.make_async_copy(near_meta, near_meta, meta_recv.at[0]).wait()
    for way in range(2):
        plane = (z + (7 if way == 0 else NZ - 7)) & (NZ - 1)
        pick = one_hot(slots_of(meta[1 + way]) == (plane << 5) + way * 16 + iota((16, ROWS), 0))
        fsend[way, 160:] = dot_nn(pick, raw[way, 0]).astype(BF16)
        far_copy(way, 5).start()

    def meta_start(pos, _):
        meta_copy(pos, 1).start()
        return 0

    lax.fori_loop(5, NZ, meta_start, 0)
    learn(3)
    tell(4)
    pack_near(0, unit)
    pack_near(1, raw.at[0, 0])
    pack_near(2, raw.at[1, 0])

    for way in range(2):
        for piece in range(pieces):
            raw_copy(way, 1, piece).wait_recv()
        slot = slots_of(meta[3 + way])
        row = iota((160, ROWS), 0)
        step = 1 + (row >> 5)
        plane = (z + (step if way == 0 else NZ - step)) & (NZ - 1)
        pick = one_hot(slot == (plane << 5) + (row & 31))
        fsend[way, :160] = dot_nn(pick, raw[way, 1]).astype(BF16)
        for g in range(5):
            far_copy(way, g).start()

    pack_near(3, raw.at[0, 1])
    pack_near(4, raw.at[1, 1])
    learn(4)

    i128 = iota((ROWS, ROWS), 0)
    lane = iota((ROWS, ROWS), 1)
    zq, j4 = (i128 >> 2) & 3, ((i128 >> 4) << 2) | (i128 & 3)

    def is_here(j):
        return jnp.logical_and(j // 2 == x, handler_y(j) == y)

    def mine16():
        return pl.ds(pl.multiple_of(xy * 16, 16), 16)

    def ext_copy(j):
        return pltpu.make_async_remote_copy(
            src_ref=pext.at[j], dst_ref=own.at[:, mine16(), pl.ds(D, EXT)],
            send_sem=ext_send.at[j], recv_sem=ext_recv,
            device_id=at(z, j // 2, c, handler_y(j)), device_id_type=MESH,
        )

    def plane_src(q, j):
        return psend.at[pl.ds(q * ROWS + pl.multiple_of(j * 16, 16), 16)]

    def plane_copy(q, j):
        return pltpu.make_async_remote_copy(
            src_ref=plane_src(q, j), dst_ref=own.at[q, mine16(), pl.ds(0, D)],
            send_sem=plane_send.at[q, j], recv_sem=own_recv.at[q, x],
            device_id=at(z, j // 2, c, handler_y(j)), device_id_type=MESH,
        )

    far_meta = meta.at[pl.ds(5, NZ - 5)]
    pltpu.make_async_copy(far_meta, far_meta, meta_recv.at[1]).wait()
    for q in range(4):
        same = jnp.zeros((ROWS, EXT), F32)
        for k in range(4):
            code = meta[q * 4 + k]
            pick = one_hot((slots_of(code) == z * 32 + j4) & (zq == k))
            same += dot_nt(pick, one_hot((((code >> 2) & 7) == i128) | (i128 == 8)))
        right = jnp.where(lane < 8, PENALTY * same - PENALTY, jnp.where(lane == 8, -PENALTY * same, 0.0))
        pext[:, q] = right.astype(BF16).reshape(8, 16, EXT)

    def ext_start(j, _):
        @pl.when(is_here(j))
        def _():
            pltpu.make_async_copy(pext.at[j], own.at[:, mine16(), pl.ds(D, EXT)], ext_recv).start()

        @pl.when(jnp.logical_not(is_here(j)))
        def _():
            ext_copy(j).start()
        return 0

    lax.fori_loop(0, 8, ext_start, 0)

    def relay(q):
        here = pl.ds(q * ROWS, ROWS)
        order = one_hot(lane == zq * 32 + j4)
        psend[here, :] = dot_nn(order, farr[here, :]).astype(BF16)

        def send(j, _):
            @pl.when(is_here(j))
            def _():
                pltpu.make_async_copy(
                    plane_src(q, j), own.at[q, mine16(), pl.ds(0, D)], own_recv.at[q, x]
                ).start()

            @pl.when(jnp.logical_not(is_here(j)))
            def _():
                plane_copy(q, j).start()
            return 0

        lax.fori_loop(0, 8, send, 0)

    def sib_copy(q, g):
        rows = pl.ds(pl.multiple_of(g * 64, 64), 64)
        return pltpu.make_async_remote_copy(
            src_ref=own.at[q, rows], dst_ref=sib.at[q, rows],
            send_sem=sib_send.at[q, g], recv_sem=sib_recv.at[q, g],
            device_id=at(z, x, 1 - c, y), device_id_type=MESH,
        )

    def terms(left_rows, right_rows):
        return jnp.exp2(dot_nt(left_rows, right_rows) * LOG2E10)

    def lane_sums(e):
        total = e[:, :128]
        for k in range(1, e.shape[1] // 128):
            total = total + e[:, k * 128 : k * 128 + 128]
        return total

    def handle(q):
        @pl.when(handles)
        def _():
            old, new = q * 256, q * 256 + 256
            if q == 0:
                lanes = own.at[:, :, pl.ds(D, EXT)]
                pltpu.make_async_copy(lanes, lanes, ext_recv).wait()

            def take(k, _):
                g = (x + k) & 3
                rows = own.at[q, pl.ds(pl.multiple_of(g * 64, 64), 64), pl.ds(0, D)]
                pltpu.make_async_copy(rows, rows, own_recv.at[q, g]).wait()
                sib_copy(q, g).start()
                return 0

            lax.fori_loop(0, 4, take, 0)
            left[old:new, :D] = own[q, :, :D]
            is_cluster = iota((256, EXT), 1) < 9
            left[old:new, D:] = jnp.where(
                is_cluster, own[q, :, D:].astype(F32) * (1.0 / PENALTY) + 1.0, 0.0
            ).astype(BF16)
            e = terms(left[:new, :], own[q])
            sums = lane_sums(e)
            acc[old:new, :] = sums[old:]
            if q:
                acc[:old, :] = acc[:old, :] + sums[:old]
                colacc[q] = jnp.sum(e[:old].reshape(old // 8, 8, 256), axis=0)
            else:
                colacc[q] = jnp.zeros((8, 256), F32)

            def sib_wait(g, _):
                sib_copy(q, g).wait_recv()
                return 0

            lax.fori_loop(0, 4, sib_wait, 0)
            acc[:new, :] = acc[:new, :] + lane_sums(terms(left[:new, :], sib[q]))
            if q:
                e = terms(left[old:new, :], sib[:q].reshape(old, WIDE))
                acc[old:new, :] = acc[old:new, :] + lane_sums(e)

    relay(0)
    for pos in (5, 6, 7):
        far_copy((pos - 5) % 2, (pos - 5) // 2).wait_recv()
    relay(1)
    handle(0)
    handle(1)
    for pos in (8, 9, 10, 11):
        far_copy((pos - 5) % 2, (pos - 5) // 2).wait_recv()
    relay(2)
    handle(2)
    for pos in (12, 13, 14):
        far_copy((pos - 5) % 2, (pos - 5) // 2).wait_recv()
    far_copy(0, 5).wait_recv()
    far_copy(1, 5).wait_recv()
    relay(3)
    handle(3)

    def tot_copy(i):
        return pltpu.make_async_remote_copy(
            src_ref=tot.at[i // 8], dst_ref=back.at[my_owner],
            send_sem=tot_send.at[i], recv_sem=tot_recv,
            device_id=at(z, i // NY, c, i % NY), device_id_type=MESH,
        )

    @pl.when(handles)
    def _():
        for q in range(4):
            for h in range(2):
                part = acc[pl.ds(q * 256 + h * 128, 128), :].T
                total = jnp.sum(part, axis=0, keepdims=True) + jnp.sum(
                    colacc[q, :, h * 128 : h * 128 + 128], axis=0, keepdims=True
                )
                tot[h, q : q + 1, :] = total
        tot[0, 4:8, :] = jnp.zeros((4, 128), F32)
        tot[1, 4:8, :] = jnp.zeros((4, 128), F32)

        def send(i, _):
            @pl.when(i == xy)
            def _():
                pltpu.make_async_copy(tot.at[i // 8], back.at[my_owner], tot_recv).start()

            @pl.when(i != xy)
            def _():
                tot_copy(i).start()
            return 0

        lax.fori_loop(0, NX * NY, send, 0)

    pltpu.make_async_copy(back, back, tot_recv).wait()
    for j in range(8):
        for q in range(4):
            ret[q, j : j + 1, :] = back[j, q : q + 1, :]

    def ret_copy(pos):
        return pltpu.make_async_remote_copy(
            src_ref=ret.at[pos // 4], dst_ref=wts.at[z],
            send_sem=ret_send.at[pos], recv_sem=ret_recv,
            device_id=at(down(pos), x, c, y), device_id_type=MESH,
        )

    def ret_start(pos, _):
        ret_copy(pos).start()
        return 0

    lax.fori_loop(1, NZ, ret_start, 0)
    wts[z] = ret[0]
    pltpu.make_async_copy(
        wts.at[pl.ds(0, NZ - 1)], wts.at[pl.ds(0, NZ - 1)], ret_recv
    ).wait()

    code = meta[0]
    table = wts[...].reshape(NZ * 8, 128).T
    lines = jnp.where((code >> 5) == iota((NZ * 8, ROWS), 0), 1.0, 0.0)
    picked = jnp.dot(table, lines, precision=lax.Precision.HIGHEST, preferred_element_type=F32)
    ahead = ((code >> 8) - z) & (NZ - 1)
    pos = jnp.where(ahead == 0, 0, jnp.where(ahead <= 8, 2 * ahead - 1, 2 * (NZ - ahead)))
    lane = (xy % 8) * 16 + (pos & 3) * 4 + (code & 3)
    total = jnp.sum(jnp.where(iota((128, ROWS), 0) == lane, picked, 0.0), axis=0, keepdims=True)
    out_ref[...] = 0.1 * jnp.log(total)

    for way in range(2):
        for hop in range(2):
            for piece in range(pieces):
                raw_copy(way, hop, piece).wait_send()
        for g in range(6):
            far_copy(way, g).wait_send()

    def drain_z(pos, _):
        meta_copy(pos, 0).wait_send()
        ret_copy(pos).wait_send()
        return 0

    lax.fori_loop(1, NZ, drain_z, 0)

    def drain_plane(j, _):
        @pl.when(jnp.logical_not(is_here(j)))
        def _():
            ext_copy(j).wait_send()
            for q in range(4):
                plane_copy(q, j).wait_send()
        return 0

    lax.fori_loop(0, 8, drain_plane, 0)

    @pl.when(handles)
    def _():
        def drain_sib(k, _):
            sib_copy(k >> 2, k & 3).wait_send()
            return 0

        lax.fori_loop(0, 16, drain_sib, 0)

        def drain_tot(i, _):
            @pl.when(i != xy)
            def _():
                tot_copy(i).wait_send()
            return 0

        lax.fori_loop(0, NX * NY, drain_tot, 0)


def per_device(embeddings, labels):
    dma = pltpu.SemaphoreType.DMA
    vmem = pltpu.VMEM
    weight = pl.pallas_call(
        kernel,
        out_shape=jax.ShapeDtypeStruct((1, ROWS), F32),
        in_specs=[pl.BlockSpec(memory_space=pl.ANY)] * 2,
        out_specs=pl.BlockSpec(memory_space=pltpu.VMEM),
        scratch_shapes=[
            vmem((ROWS, D), BF16),
            vmem((1, ROWS), jnp.int32),
            vmem((ROWS, D), BF16),
            vmem((2, 2, ROWS, D), BF16),
            vmem((2, 176, D), BF16),
            vmem((NZ * 32, D), BF16),
            vmem((NZ, 1, ROWS), jnp.int32),
            vmem((4 * ROWS, D), BF16),
            vmem((8, 4, 16, EXT), BF16),
            vmem((4, 256, WIDE), BF16),
            vmem((4, 256, WIDE), BF16),
            vmem((1024, WIDE), BF16),
            vmem((1024, 128), F32),
            vmem((4, 8, 256), F32),
            vmem((2, 8, 128), F32),
            vmem((8, 8, 128), F32),
            vmem((4, 8, 128), F32),
            vmem((NZ, 8, 128), F32),
            dma((2,)), pltpu.SemaphoreType.REGULAR((5,)),
            dma((2, 2, ROWS // PIECE)), dma((2, 2, ROWS // PIECE)),
            dma((2, 6)), dma((17,)),
            dma((NZ,)), dma((2,)),
            dma((4, 8)), dma((4, 4)),
            dma((8,)), dma,
            dma((4, 4)), dma((4, 4)),
            dma((NX * NY,)), dma,
            dma((NZ,)), dma,
        ],
        compiler_params=pltpu.CompilerParams(
            collective_id=0, has_side_effects=True, vmem_limit_bytes=40 * 1024 * 1024
        ),
        name="soft_dedup",
    )(embeddings, labels.reshape(1, ROWS))
    return weight.reshape(ROWS)


def solution(mesh):
    placed = (P(("shard", "split"), None), P(("shard", "split")))
    return jax.shard_map(
        per_device, mesh=mesh, in_specs=placed, out_specs=P(("shard", "split")), check_vma=False
    )
```

time: 82.6 us -> 80.5 us (0.975)
  Pallas kernels: 80.3 us -> 78.2 us
    pallas_call x1, Pallas kernels: 80.3 us -> 78.2 us  [per_device(): pl.pallas_call(kernel, out_shape=jax.ShapeDtypeStruct((1, ROWS), F32), in...]
where the time goes in v2:
time: 80.5 us; the launch traced here: 80.3 us
  Pallas kernels  78.2 us (97%)
  local copies, waits for them, and re-layouts  2.09 us (3%)
    pallas_call x1, Pallas kernels, per_device(): pl.pallas_call(kernel, out_shape=jax.ShapeDtypeStruct((1, ROWS), F32), in...  78.2 us
    unnamed x5, local copies, waits for them, and re-layouts  2.09 us

profile of v2, /device:TPU:1, one launch (start us, length us, event | category | flops | bytes accessed | tf_op | source)
XLA Modules:
  0.0 80.3 jit_solution(6131577180114153664)
XLA Ops:
  0.0 0.0 copy-start.1
  0.0 0.7 copy-done.1
  0.7 0.0 copy-start
  0.7 0.9 %copy-done = bf16[128,768]{1,0:T(8,128)(2,1)S(1)} copy-done((bf16[128,768]{1,0:T(8,128)(2,1)S(1)}, bf16[128,768]{1,0:T(8,128)(2,1)}, u32[]{:S(2)}) %copy-start) | copy-done | bytes 196632
  1.6 78.2 %soft_dedup.1 = f32[1,128]{1,0:T(1,128)S(1)} custom-call(bf16[128,768]{1,0:T(8,128)(2,1)S(1)} %copy-done, s32[1,128]{1,0:T(1,128)S(1)} %bitcast.2), custom_call_target="tpu_custom_call" | custom-call | tf_op jit(solution)/shard_map/soft_dedup/pallas_call | solution.py:457
  79.8 0.5 copy.4
Async XLA Ops:
  0.0 0.7 copy-start.1
  0.7 0.9 %copy-start = (bf16[128,768]{1,0:T(8,128)(2,1)S(1)}, bf16[128,768]{1,0:T(8,128)(2,1)}, u32[]{:S(2)}) copy-start(bf16[128,768]{1,0:T(8,128)(2,1)} %emb_hbm.1) | copy-start | bytes 589828

commit v3 on v2

--- a/solution.py
+++ b/solution.py
@@ -39,8 +39,9 @@
 
 def kernel(
     emb_hbm, lab_hbm, out_ref,
-    emb, lab, unit, raw, fsend, farr, meta, psend, pext, own, sib, left, acc, colacc, tot, back, ret, wts,
-    in_sem, known, raw_send, raw_recv, far_send, far_recv, meta_send, meta_recv, plane_send, own_recv,
+    emb, lab, unit, raw, meta, near_out, far_out, opp_out, blocks, pext, ext_in, own, sib, left, acc, colacc,
+    tot, back, ret, wts,
+    in_sem, known, raw_send, raw_recv, near_send, far_send, opp_send, meta_send, meta_recv, own_recv,
     ext_send, ext_recv, sib_send, sib_recv, tot_send, tot_recv, ret_send, ret_recv,
 ):
     p = lax.axis_index("shard")
@@ -143,24 +144,56 @@
     def slots_of(code):
         return ((code >> 5) << 2) | (code & 3)
 
-    def pack_near(pos, rows_ref):
-        slot = slots_of(meta[pos])
-        pick = one_hot(slot == z * 32 + iota((32, ROWS), 0))
-        farr[pl.ds(pos * 32, 32), :] = dot_nn(pick, rows_ref[...]).astype(BF16)
-
-    def far_copy(way, g):
-        step = 1 + g if g < 5 else 7
-        to = (z + (step if way == 0 else NZ - step)) & (NZ - 1)
-        if g < 5:
-            pos = 2 * g + 5 + way
-            src, dst, sem = fsend.at[way, pl.ds(g * 32, 32)], farr.at[pl.ds(pos * 32, 32)], pos
-        else:
-            src = fsend.at[way, pl.ds(160, 16)]
-            dst, sem = farr.at[pl.ds(480 + way * 16, 16)], 15 + way
-        return pltpu.make_async_remote_copy(
-            src_ref=src, dst_ref=dst, send_sem=far_send.at[way, g], recv_sem=far_recv.at[sem],
-            device_id=at(to, x, c, y), device_id_type=MESH,
-        )
+    def to_blocks(code, first, count, rows):
+        line = iota((8 * count, ROWS), 0)
+        pick = one_hot(slots_of(code) == ((first(line >> 3) << 2) | (line & 3)))
+        twice = dot_nn(pick, rows)
+        upper = (iota((8 * count, 128), 0) & 4) == 0
+        thirds = [
+            jnp.where(upper, twice[:, k : k + 128], twice[:, k + 128 : k + 256]).reshape(count, 8, 128)
+            for k in range(0, D, 256)
+        ]
+        return jnp.concatenate(thirds, axis=1).astype(BF16)
+
+    def is_here(j):
+        return jnp.logical_and(j // 2 == x, handler_y(j) == y)
+
+    def handler(zz, j):
+        return at(zz, j // 2, c, handler_y(j))
+
+    def block_copy(src, pos, zz, j, sem):
+        return pltpu.make_async_remote_copy(
+            src_ref=src, dst_ref=blocks.at[pos, xy], send_sem=sem, recv_sem=own_recv.at[pos],
+            device_id=handler(zz, j), device_id_type=MESH,
+        )
+
+    def near_copy(pos, j):
+        return block_copy(near_out.at[pos, j], pos, z, j, near_send.at[pos, j])
+
+    def far_plane(way, g):
+        return (z + (1 + g if way == 0 else NZ - 1 - g)) & (NZ - 1)
+
+    def far_copy(way, g, j):
+        return block_copy(far_out.at[way, g * 8 + j], 2 * g + 5 + way, far_plane(way, g), j, far_send.at[way])
+
+    def opp_copy(way, j):
+        zz = (z + (7 if way == 0 else NZ - 7)) & (NZ - 1)
+        return block_copy(opp_out.at[way, j], 15, zz, way * 4 + j, opp_send.at[way])
+
+    def send_near(pos, rows_ref):
+        near_out[pos] = to_blocks(meta[pos], lambda j: z * 8 + j, 8, rows_ref[...])
+
+        def send(j, _):
+            @pl.when(is_here(j))
+            def _():
+                pltpu.make_async_copy(near_out.at[pos, j], blocks.at[pos, xy], own_recv.at[pos]).start()
+
+            @pl.when(jnp.logical_not(is_here(j)))
+            def _():
+                near_copy(pos, j).start()
+            return 0
+
+        lax.fori_loop(0, 8, send, 0)
 
     for piece in range(pieces):
         for way in range(2):
@@ -171,63 +204,56 @@
             tell(3)
     near_meta = meta.at[pl.ds(1, 4)]
     pltpu.make_async_copy(near_meta, near_meta, meta_recv.at[0]).wait()
-    for way in range(2):
-        plane = (z + (7 if way == 0 else NZ - 7)) & (NZ - 1)
-        pick = one_hot(slots_of(meta[1 + way]) == (plane << 5) + way * 16 + iota((16, ROWS), 0))
-        fsend[way, 160:] = dot_nn(pick, raw[way, 0]).astype(BF16)
-        far_copy(way, 5).start()
+    learn(3)
+    tell(4)
 
     def meta_start(pos, _):
         meta_copy(pos, 1).start()
         return 0
 
     lax.fori_loop(5, NZ, meta_start, 0)
-    learn(3)
-    tell(4)
-    pack_near(0, unit)
-    pack_near(1, raw.at[0, 0])
-    pack_near(2, raw.at[1, 0])
+    for way in range(2):
+        zz = (z + (7 if way == 0 else NZ - 7)) & (NZ - 1)
+        first = functools.partial(lambda base, j: base + j, zz * 8 + way * 4)
+        opp_out[way] = to_blocks(meta[1 + way], first, 4, raw[way, 0])
+    learn(4)
+    for way in range(2):
+        for j in range(4):
+            opp_copy(way, j).start()
+    send_near(0, unit)
 
     for way in range(2):
         for piece in range(pieces):
             raw_copy(way, 1, piece).wait_recv()
-        slot = slots_of(meta[3 + way])
-        row = iota((160, ROWS), 0)
-        step = 1 + (row >> 5)
-        plane = (z + (step if way == 0 else NZ - step)) & (NZ - 1)
-        pick = one_hot(slot == (plane << 5) + (row & 31))
-        fsend[way, :160] = dot_nn(pick, raw[way, 1]).astype(BF16)
-        for g in range(5):
-            far_copy(way, g).start()
-
-    pack_near(3, raw.at[0, 1])
-    pack_near(4, raw.at[1, 1])
-    learn(4)
+
+        def first(i, way=way):
+            step = 1 + (i >> 3)
+            return (((z + (step if way == 0 else NZ - step)) & (NZ - 1)) << 3) + (i & 7)
+
+        far_out[way] = to_blocks(meta[3 + way], first, 40, raw[way, 1])
+    for g in range(5):
+        for way in range(2):
+            def far_start(j, _, g=g, way=way):
+                far_copy(way, g, j).start()
+                return 0
+
+            lax.fori_loop(0, 8, far_start, 0)
+    send_near(1, raw.at[0, 0])
+    send_near(2, raw.at[1, 0])
+    send_near(3, raw.at[0, 1])
+    send_near(4, raw.at[1, 1])
 
     i128 = iota((ROWS, ROWS), 0)
     lane = iota((ROWS, ROWS), 1)
     zq, j4 = (i128 >> 2) & 3, ((i128 >> 4) << 2) | (i128 & 3)
 
-    def is_here(j):
-        return jnp.logical_and(j // 2 == x, handler_y(j) == y)
-
     def mine16():
         return pl.ds(pl.multiple_of(xy * 16, 16), 16)
 
     def ext_copy(j):
         return pltpu.make_async_remote_copy(
-            src_ref=pext.at[j], dst_ref=own.at[:, mine16(), pl.ds(D, EXT)],
+            src_ref=pext.at[j], dst_ref=ext_in.at[:, mine16()],
             send_sem=ext_send.at[j], recv_sem=ext_recv,
-            device_id=at(z, j // 2, c, handler_y(j)), device_id_type=MESH,
-        )
-
-    def plane_src(q, j):
-        return psend.at[pl.ds(q * ROWS + pl.multiple_of(j * 16, 16), 16)]
-
-    def plane_copy(q, j):
-        return pltpu.make_async_remote_copy(
-            src_ref=plane_src(q, j), dst_ref=own.at[q, mine16(), pl.ds(0, D)],
-            send_sem=plane_send.at[q, j], recv_sem=own_recv.at[q, x],
             device_id=at(z, j // 2, c, handler_y(j)), device_id_type=MESH,
         )
 
@@ -245,7 +271,7 @@
     def ext_start(j, _):
         @pl.when(is_here(j))
         def _():
-            pltpu.make_async_copy(pext.at[j], own.at[:, mine16(), pl.ds(D, EXT)], ext_recv).start()
+            pltpu.make_async_copy(pext.at[j], ext_in.at[:, mine16()], ext_recv).start()
 
         @pl.when(jnp.logical_not(is_here(j)))
         def _():
@@ -253,25 +279,6 @@
         return 0
 
     lax.fori_loop(0, 8, ext_start, 0)
-
-    def relay(q):
-        here = pl.ds(q * ROWS, ROWS)
-        order = one_hot(lane == zq * 32 + j4)
-        psend[here, :] = dot_nn(order, farr[here, :]).astype(BF16)
-
-        def send(j, _):
-            @pl.when(is_here(j))
-            def _():
-                pltpu.make_async_copy(
-                    plane_src(q, j), own.at[q, mine16(), pl.ds(0, D)], own_recv.at[q, x]
-                ).start()
-
-            @pl.when(jnp.logical_not(is_here(j)))
-            def _():
-                plane_copy(q, j).start()
-            return 0
-
-        lax.fori_loop(0, 8, send, 0)
 
     def sib_copy(q, g):
         rows = pl.ds(pl.multiple_of(g * 64, 64), 64)
@@ -295,14 +302,25 @@
         def _():
             old, new = q * 256, q * 256 + 256
             if q == 0:
-                lanes = own.at[:, :, pl.ds(D, EXT)]
-                pltpu.make_async_copy(lanes, lanes, ext_recv).wait()
+                pltpu.make_async_copy(ext_in, ext_in, ext_recv).wait()
+                row, col = iota((256, 256), 0), iota((256, 256), 1)
+                order = one_hot(col == (((row >> 2) & 15) << 4) + ((row >> 6) << 2) + (row & 3))
+                for k in range(4):
+                    own[k, :, D:] = dot_nn(order, ext_in[k]).astype(BF16)
+
+            row, col = iota((384, 384), 0), iota((384, 384), 1)
+            line = ((row >> 2) & 15) * 24 + ((row >> 6) << 2) + (row & 3)
+            unpack = one_hot(col == line)
 
             def take(k, _):
-                g = (x + k) & 3
-                rows = own.at[q, pl.ds(pl.multiple_of(g * 64, 64), 64), pl.ds(0, D)]
-                pltpu.make_async_copy(rows, rows, own_recv.at[q, g]).wait()
-                sib_copy(q, g).start()
+                pos = q * 4 + k
+                pltpu.make_async_copy(blocks.at[pos], blocks.at[pos], own_recv.at[pos]).wait()
+                lines = blocks[pos].astype(F32).reshape(384, 128).astype(BF16)
+                parts = dot_nn(unpack, lines).astype(BF16)
+                here = pl.ds(pl.multiple_of(k * 64, 64), 64)
+                for i in range(6):
+                    own[q, here, i * 128 : i * 128 + 128] = parts[i * 64 : i * 64 + 64]
+                sib_copy(q, k).start()
                 return 0
 
             lax.fori_loop(0, 4, take, 0)
@@ -330,26 +348,12 @@
                 e = terms(left[old:new, :], sib[:q].reshape(old, WIDE))
                 acc[old:new, :] = acc[old:new, :] + lane_sums(e)
 
-    relay(0)
-    for pos in (5, 6, 7):
-        far_copy((pos - 5) % 2, (pos - 5) // 2).wait_recv()
-    relay(1)
-    handle(0)
-    handle(1)
-    for pos in (8, 9, 10, 11):
-        far_copy((pos - 5) % 2, (pos - 5) // 2).wait_recv()
-    relay(2)
-    handle(2)
-    for pos in (12, 13, 14):
-        far_copy((pos - 5) % 2, (pos - 5) // 2).wait_recv()
-    far_copy(0, 5).wait_recv()
-    far_copy(1, 5).wait_recv()
-    relay(3)
-    handle(3)
+    for q in range(4):
+        handle(q)
 
     def tot_copy(i):
         return pltpu.make_async_remote_copy(
-            src_ref=tot.at[i // 8], dst_ref=back.at[my_owner],
+            src_ref=tot, dst_ref=back.at[my_owner],
             send_sem=tot_send.at[i], recv_sem=tot_recv,
             device_id=at(z, i // NY, c, i % NY), device_id_type=MESH,
         )
@@ -362,14 +366,12 @@
                 total = jnp.sum(part, axis=0, keepdims=True) + jnp.sum(
                     colacc[q, :, h * 128 : h * 128 + 128], axis=0, keepdims=True
                 )
-                tot[h, q : q + 1, :] = total
-        tot[0, 4:8, :] = jnp.zeros((4, 128), F32)
-        tot[1, 4:8, :] = jnp.zeros((4, 128), F32)
+                tot[q * 2 + h : q * 2 + h + 1, :] = total
 
         def send(i, _):
             @pl.when(i == xy)
             def _():
-                pltpu.make_async_copy(tot.at[i // 8], back.at[my_owner], tot_recv).start()
+                pltpu.make_async_copy(tot, back.at[my_owner], tot_recv).start()
 
             @pl.when(i != xy)
             def _():
@@ -380,12 +382,12 @@
 
     pltpu.make_async_copy(back, back, tot_recv).wait()
     for j in range(8):
-        for q in range(4):
-            ret[q, j : j + 1, :] = back[j, q : q + 1, :]
+        for k in range(8):
+            ret[k, j : j + 1, :] = back[j, k : k + 1, :]
 
     def ret_copy(pos):
         return pltpu.make_async_remote_copy(
-            src_ref=ret.at[pos // 4], dst_ref=wts.at[z],
+            src_ref=ret.at[pos // 2], dst_ref=wts.at[z],
             send_sem=ret_send.at[pos], recv_sem=ret_recv,
             device_id=at(down(pos), x, c, y), device_id_type=MESH,
         )
@@ -406,7 +408,7 @@
     picked = jnp.dot(table, lines, precision=lax.Precision.HIGHEST, preferred_element_type=F32)
     ahead = ((code >> 8) - z) & (NZ - 1)
     pos = jnp.where(ahead == 0, 0, jnp.where(ahead <= 8, 2 * ahead - 1, 2 * (NZ - ahead)))
-    lane = (xy % 8) * 16 + (pos & 3) * 4 + (code & 3)
+    lane = (pos & 1) * 64 + xy * 4 + (code & 3)
     total = jnp.sum(jnp.where(iota((128, ROWS), 0) == lane, picked, 0.0), axis=0, keepdims=True)
     out_ref[...] = 0.1 * jnp.log(total)
 
@@ -414,8 +416,8 @@
         for hop in range(2):
             for piece in range(pieces):
                 raw_copy(way, hop, piece).wait_send()
-        for g in range(6):
-            far_copy(way, g).wait_send()
+        pltpu.make_async_copy(far_out.at[way], far_out.at[way], far_send.at[way]).wait()
+        pltpu.make_async_copy(opp_out.at[way], opp_out.at[way], opp_send.at[way]).wait()
 
     def drain_z(pos, _):
         meta_copy(pos, 0).wait_send()
@@ -428,8 +430,8 @@
         @pl.when(jnp.logical_not(is_here(j)))
         def _():
             ext_copy(j).wait_send()
-            for q in range(4):
-                plane_copy(q, j).wait_send()
+            for pos in range(5):
+                near_copy(pos, j).wait_send()
         return 0
 
     lax.fori_loop(0, 8, drain_plane, 0)
@@ -457,32 +459,34 @@
     weight = pl.pallas_call(
         kernel,
         out_shape=jax.ShapeDtypeStruct((1, ROWS), F32),
-        in_specs=[pl.BlockSpec(memory_space=pl.ANY)] * 2,
+        in_specs=[pl.BlockSpec(memory_space=pltpu.HBM)] * 2,
         out_specs=pl.BlockSpec(memory_space=pltpu.VMEM),
         scratch_shapes=[
             vmem((ROWS, D), BF16),
             vmem((1, ROWS), jnp.int32),
             vmem((ROWS, D), BF16),
             vmem((2, 2, ROWS, D), BF16),
-            vmem((2, 176, D), BF16),
-            vmem((NZ * 32, D), BF16),
             vmem((NZ, 1, ROWS), jnp.int32),
-            vmem((4 * ROWS, D), BF16),
+            vmem((5, 8, 24, 128), BF16),
+            vmem((2, 40, 24, 128), BF16),
+            vmem((2, 4, 24, 128), BF16),
+            vmem((NZ, 16, 24, 128), BF16),
             vmem((8, 4, 16, EXT), BF16),
+            vmem((4, 256, EXT), BF16),
             vmem((4, 256, WIDE), BF16),
             vmem((4, 256, WIDE), BF16),
             vmem((1024, WIDE), BF16),
             vmem((1024, 128), F32),
             vmem((4, 8, 256), F32),
-            vmem((2, 8, 128), F32),
+            vmem((8, 128), F32),
             vmem((8, 8, 128), F32),
-            vmem((4, 8, 128), F32),
+            vmem((8, 8, 128), F32),
             vmem((NZ, 8, 128), F32),
             dma((2,)), pltpu.SemaphoreType.REGULAR((5,)),
             dma((2, 2, ROWS // PIECE)), dma((2, 2, ROWS // PIECE)),
-            dma((2, 6)), dma((17,)),
+            dma((5, 8)), dma((2,)), dma((2,)),
             dma((NZ,)), dma((2,)),
-            dma((4, 8)), dma((4, 4)),
+            dma((NZ,)),
             dma((8,)), dma,
             dma((4, 4)), dma((4, 4)),
             dma((NX * NY,)), dma,

time: 80.5 us -> 74.6 us (0.927)
  Pallas kernels: 78.2 us -> 72 us
    pallas_call x1, Pallas kernels: 78.2 us -> 72 us  [per_device(): pl.pallas_call(kernel, out_shape=jax.ShapeDtypeStruct((1, ROWS), F32), in...]
where the time goes in v3:
time: 74.6 us; the launch traced here: 74.1 us
  Pallas kernels  72 us (97%)
  local copies, waits for them, and re-layouts  2.09 us (3%)
    pallas_call x1, Pallas kernels, per_device(): pl.pallas_call(kernel, out_shape=jax.ShapeDtypeStruct((1, ROWS), F32), in...  72 us
    unnamed x5, local copies, waits for them, and re-layouts  2.09 us

profile of v3, /device:TPU:1, one launch (start us, length us, event | category | flops | bytes accessed | tf_op | source)
XLA Modules:
  0.0 74.1 jit_solution(9725312479921332990)
XLA Ops:
  0.0 0.0 copy-start.1
  0.0 0.7 copy-done.1
  0.7 0.0 copy-start
  0.7 0.9 %copy-done = bf16[128,768]{1,0:T(8,128)(2,1)S(1)} copy-done((bf16[128,768]{1,0:T(8,128)(2,1)S(1)}, bf16[128,768]{1,0:T(8,128)(2,1)}, u32[]{:S(2)}) %copy-start) | copy-done | bytes 196632
  1.6 72.0 %soft_dedup.1 = f32[1,128]{1,0:T(1,128)S(1)} custom-call(bf16[128,768]{1,0:T(8,128)(2,1)S(1)} %copy-done, s32[1,128]{1,0:T(1,128)S(1)} %bitcast.2), custom_call_target="tpu_custom_call" | custom-call | tf_op jit(solution)/shard_map/soft_dedup/pallas_call | solution.py:459
  73.6 0.5 copy.4
Async XLA Ops:
  0.0 0.7 copy-start.1
  0.7 0.9 %copy-start = (bf16[128,768]{1,0:T(8,128)(2,1)S(1)}, bf16[128,768]{1,0:T(8,128)(2,1)}, u32[]{:S(2)}) copy-start(bf16[128,768]{1,0:T(8,128)(2,1)} %emb_hbm.1) | copy-start | bytes 589828

commit v4 on v3

--- a/solution.py
+++ b/solution.py
@@ -297,59 +297,75 @@
             total = total + e[:, k * 128 : k * 128 + 128]
         return total
 
-    def handle(q):
-        @pl.when(handles)
-        def _():
-            old, new = q * 256, q * 256 + 256
-            if q == 0:
-                pltpu.make_async_copy(ext_in, ext_in, ext_recv).wait()
-                row, col = iota((256, 256), 0), iota((256, 256), 1)
-                order = one_hot(col == (((row >> 2) & 15) << 4) + ((row >> 6) << 2) + (row & 3))
-                for k in range(4):
-                    own[k, :, D:] = dot_nn(order, ext_in[k]).astype(BF16)
-
-            row, col = iota((384, 384), 0), iota((384, 384), 1)
-            line = ((row >> 2) & 15) * 24 + ((row >> 6) << 2) + (row & 3)
-            unpack = one_hot(col == line)
-
-            def take(k, _):
-                pos = q * 4 + k
-                pltpu.make_async_copy(blocks.at[pos], blocks.at[pos], own_recv.at[pos]).wait()
-                lines = blocks[pos].astype(F32).reshape(384, 128).astype(BF16)
-                parts = dot_nn(unpack, lines).astype(BF16)
-                here = pl.ds(pl.multiple_of(k * 64, 64), 64)
-                for i in range(6):
-                    own[q, here, i * 128 : i * 128 + 128] = parts[i * 64 : i * 64 + 64]
-                sib_copy(q, k).start()
-                return 0
-
-            lax.fori_loop(0, 4, take, 0)
-            left[old:new, :D] = own[q, :, :D]
-            is_cluster = iota((256, EXT), 1) < 9
-            left[old:new, D:] = jnp.where(
-                is_cluster, own[q, :, D:].astype(F32) * (1.0 / PENALTY) + 1.0, 0.0
-            ).astype(BF16)
-            e = terms(left[:new, :], own[q])
-            sums = lane_sums(e)
-            acc[old:new, :] = sums[old:]
-            if q:
-                acc[:old, :] = acc[:old, :] + sums[:old]
-                colacc[q] = jnp.sum(e[:old].reshape(old // 8, 8, 256), axis=0)
-            else:
-                colacc[q] = jnp.zeros((8, 256), F32)
-
-            def sib_wait(g, _):
-                sib_copy(q, g).wait_recv()
-                return 0
-
-            lax.fori_loop(0, 4, sib_wait, 0)
-            acc[:new, :] = acc[:new, :] + lane_sums(terms(left[:new, :], sib[q]))
-            if q:
-                e = terms(left[old:new, :], sib[:q].reshape(old, WIDE))
-                acc[old:new, :] = acc[old:new, :] + lane_sums(e)
-
-    for q in range(4):
-        handle(q)
+    def permute_lanes():
+        pltpu.make_async_copy(ext_in, ext_in, ext_recv).wait()
+        row, col = iota((256, 256), 0), iota((256, 256), 1)
+        order = one_hot(col == (((row >> 2) & 15) << 4) + ((row >> 6) << 2) + (row & 3))
+        for k in range(4):
+            own[k, :, D:] = dot_nn(order, ext_in[k]).astype(BF16)
+
+    def take(q):
+        row, col = iota((384, 384), 0), iota((384, 384), 1)
+        line = ((row >> 2) & 15) * 24 + ((row >> 6) << 2) + (row & 3)
+        unpack = one_hot(col == line)
+
+        def one(k, _):
+            pos = q * 4 + k
+            pltpu.make_async_copy(blocks.at[pos], blocks.at[pos], own_recv.at[pos]).wait()
+            lines = blocks[pos].astype(F32).reshape(384, 128).astype(BF16)
+            parts = dot_nn(unpack, lines).astype(BF16)
+            here = pl.ds(pl.multiple_of(k * 64, 64), 64)
+            for i in range(6):
+                own[q, here, i * 128 : i * 128 + 128] = parts[i * 64 : i * 64 + 64]
+            sib_copy(q, k).start()
+            return 0
+
+        lax.fori_loop(0, 4, one, 0)
+
+    def own_sums(q):
+        old, new = q * 256, q * 256 + 256
+        left[old:new, :D] = own[q, :, :D]
+        is_cluster = iota((256, EXT), 1) < 9
+        left[old:new, D:] = jnp.where(
+            is_cluster, own[q, :, D:].astype(F32) * (1.0 / PENALTY) + 1.0, 0.0
+        ).astype(BF16)
+        e = terms(left[:new, :], own[q])
+        sums = lane_sums(e)
+        acc[old:new, :] = sums[old:]
+        if q:
+            acc[:old, :] = acc[:old, :] + sums[:old]
+            colacc[q] = jnp.sum(e[:old].reshape(old // 8, 8, 256), axis=0)
+        else:
+            colacc[q] = jnp.zeros((8, 256), F32)
+
+    def sib_sums(q):
+        old, new = q * 256, q * 256 + 256
+
+        def sib_wait(g, _):
+            sib_copy(q, g).wait_recv()
+            return 0
+
+        lax.fori_loop(0, 4, sib_wait, 0)
+        acc[:new, :] = acc[:new, :] + lane_sums(terms(left[:new, :], sib[q]))
+        if q:
+            e = terms(left[old:new, :], sib[:q].reshape(old, WIDE))
+            acc[old:new, :] = acc[old:new, :] + lane_sums(e)
+
+    @pl.when(handles)
+    def _():
+        permute_lanes()
+        take(0)
+        take(1)
+        own_sums(0)
+        own_sums(1)
+        take(2)
+        own_sums(2)
+        sib_sums(0)
+        sib_sums(1)
+        take(3)
+        sib_sums(2)
+        own_sums(3)
+        sib_sums(3)
 
     def tot_copy(i):
         return pltpu.make_async_remote_copy(
@@ -493,7 +509,7 @@
             dma((NZ,)), dma,
         ],
         compiler_params=pltpu.CompilerParams(
-            collective_id=0, has_side_effects=True, vmem_limit_bytes=40 * 1024 * 1024
+            collective_id=0, has_side_effects=True, vmem_limit_bytes=64 * 1024 * 1024
         ),
         name="soft_dedup",
     )(embeddings, labels.reshape(1, ROWS))

time: 74.6 us -> 71.3 us (0.956)
  Pallas kernels: 72 us -> 69.6 us
  local copies, waits for them, and re-layouts: 2.09 us -> 1.1 us
    pallas_call x1, Pallas kernels: 72 us -> 69.6 us  [per_device(): pl.pallas_call(kernel, out_shape=jax.ShapeDtypeStruct((1, ROWS), F32), in...]
    unnamed x5 -> x3, local copies, waits for them, and re-layouts: 2.09 us -> 1.1 us
where the time goes in v4:
time: 71.3 us; the launch traced here: 70.7 us
  Pallas kernels  69.6 us (98%)
  local copies, waits for them, and re-layouts  1.1 us (2%)
    pallas_call x1, Pallas kernels, per_device(): pl.pallas_call(kernel, out_shape=jax.ShapeDtypeStruct((1, ROWS), F32), in...  69.6 us

profile of v4, /device:TPU:1, one launch (start us, length us, event | category | flops | bytes accessed | tf_op | source)
XLA Modules:
  0.0 70.7 jit_solution(3848352262479755735)
XLA Ops:
  0.0 69.6 %soft_dedup.1 = f32[1,128]{1,0:T(1,128)} custom-call(bf16[128,768]{1,0:T(8,128)(2,1)} %emb_hbm.1, s32[1,128]{1,0:T(1,128)} %bitcast.2), custom_call_target="tpu_custom_call" | custom-call | tf_op jit(solution)/shard_map/soft_dedup/pallas_call | solution.py:475
  69.6 0.0 copy-start
  69.6 0.6 copy-done
  70.2 0.5 copy.4
Async XLA Ops:
  69.6 0.6 copy-start

commit v5 on v4

--- a/solution.py
+++ b/solution.py
@@ -33,6 +33,10 @@
     return lax.dot_general(a, b, (((1,), (1,)), ((), ())), preferred_element_type=F32)
 
 
+def seat(pos):
+    return jnp.where(pos < 5, pos, 20 - pos) if not isinstance(pos, int) else pos if pos < 5 else 20 - pos
+
+
 def iota(shape, dim):
     return lax.broadcasted_iota(jnp.int32, shape, dim)
 
@@ -40,33 +44,33 @@
 def kernel(
     emb_hbm, lab_hbm, out_ref,
     emb, lab, unit, raw, meta, near_out, far_out, opp_out, blocks, pext, ext_in, own, sib, left, acc, colacc,
-    tot, back, ret, wts,
+    tot, wts,
     in_sem, known, raw_send, raw_recv, near_send, far_send, opp_send, meta_send, meta_recv, own_recv,
-    ext_send, ext_recv, sib_send, sib_recv, tot_send, tot_recv, ret_send, ret_recv,
+    ext_send, ext_recv, sib_send, sib_recv, tot_send, tot_recv,
 ):
     p = lax.axis_index("shard")
     y = lax.axis_index("split")
-    z = p // 8
-    x = (p % 8) // 2
-    c = p % 2
+    z = p >> 3
+    x = (p >> 1) & 3
+    c = p & 1
     xy = x * NY + y
-    turn = (y - x + NY) % NY
-    handles = turn % 2 == 0
-    my_owner = x * 2 + turn // 2
+    turn = (y - x + NY) & 3
+    handles = (turn & 1) == 0
+    my_owner = x * 2 + (turn >> 1)
 
     def at(zz, xx, cc, yy):
         return (zz * 8 + xx * 2 + cc, yy)
 
     def handler_y(j):
-        return (2 * (j % 2) + j // 2) % NY
+        return (2 * (j & 1) + (j >> 1)) & 3
 
     def up(pos):
-        k = (pos + 1) // 2
-        return (z + jnp.where(pos % 2 == 1, k, NZ - k)) % NZ
+        k = (pos + 1) >> 1
+        return (z + jnp.where((pos & 1) == 1, k, NZ - k)) & (NZ - 1)
 
     def down(pos):
-        k = (pos + 1) // 2
-        return (z + jnp.where(pos % 2 == 1, NZ - k, k)) % NZ
+        k = (pos + 1) >> 1
+        return (z + jnp.where((pos & 1) == 1, NZ - k, k)) & (NZ - 1)
 
     barrier = pltpu.get_barrier_semaphore()
     z_by = lambda k: at((z + k + NZ) & (NZ - 1), x, c, y)
@@ -112,7 +116,7 @@
     def raw_copy(way, hop, piece):
         rows = pl.ds(piece * PIECE, PIECE)
         src = unit.at[rows] if hop == 0 else raw.at[way, 0, rows]
-        to = (z + (1 if way == 0 else NZ - 1)) % NZ
+        to = (z + (1 if way == 0 else NZ - 1)) & (NZ - 1)
         return pltpu.make_async_remote_copy(
             src_ref=src, dst_ref=raw.at[way, hop, rows],
             send_sem=raw_send.at[way, hop, piece], recv_sem=raw_recv.at[way, hop, piece],
@@ -156,10 +160,10 @@
         return jnp.concatenate(thirds, axis=1).astype(BF16)
 
     def is_here(j):
-        return jnp.logical_and(j // 2 == x, handler_y(j) == y)
+        return jnp.logical_and((j >> 1) == x, handler_y(j) == y)
 
     def handler(zz, j):
-        return at(zz, j // 2, c, handler_y(j))
+        return at(zz, (j >> 1), c, handler_y(j))
 
     def block_copy(src, pos, zz, j, sem):
         return pltpu.make_async_remote_copy(
@@ -231,13 +235,17 @@
             return (((z + (step if way == 0 else NZ - step)) & (NZ - 1)) << 3) + (i & 7)
 
         far_out[way] = to_blocks(meta[3 + way], first, 40, raw[way, 1])
-    for g in range(5):
+
+    def send_far(g):
         for way in range(2):
-            def far_start(j, _, g=g, way=way):
+            def far_start(j, _, way=way):
                 far_copy(way, g, j).start()
                 return 0
 
             lax.fori_loop(0, 8, far_start, 0)
+
+    for g in (4, 3, 2, 1, 0):
+        send_far(g)
     send_near(1, raw.at[0, 0])
     send_near(2, raw.at[1, 0])
     send_near(3, raw.at[0, 1])
@@ -254,7 +262,7 @@
         return pltpu.make_async_remote_copy(
             src_ref=pext.at[j], dst_ref=ext_in.at[:, mine16()],
             send_sem=ext_send.at[j], recv_sem=ext_recv,
-            device_id=at(z, j // 2, c, handler_y(j)), device_id_type=MESH,
+            device_id=at(z, (j >> 1), c, handler_y(j)), device_id_type=MESH,
         )
 
     far_meta = meta.at[pl.ds(5, NZ - 5)]
@@ -262,7 +270,7 @@
     for q in range(4):
         same = jnp.zeros((ROWS, EXT), F32)
         for k in range(4):
-            code = meta[q * 4 + k]
+            code = meta[seat(q * 4 + k)]
             pick = one_hot((slots_of(code) == z * 32 + j4) & (zq == k))
             same += dot_nt(pick, one_hot((((code >> 2) & 7) == i128) | (i128 == 8)))
         right = jnp.where(lane < 8, PENALTY * same - PENALTY, jnp.where(lane == 8, -PENALTY * same, 0.0))
@@ -310,7 +318,7 @@
         unpack = one_hot(col == line)
 
         def one(k, _):
-            pos = q * 4 + k
+            pos = seat(q * 4 + k)
             pltpu.make_async_copy(blocks.at[pos], blocks.at[pos], own_recv.at[pos]).wait()
             lines = blocks[pos].astype(F32).reshape(384, 128).astype(BF16)
             parts = dot_nn(unpack, lines).astype(BF16)
@@ -358,9 +366,9 @@
         take(1)
         own_sums(0)
         own_sums(1)
+        sib_sums(0)
         take(2)
         own_sums(2)
-        sib_sums(0)
         sib_sums(1)
         take(3)
         sib_sums(2)
@@ -368,10 +376,11 @@
         sib_sums(3)
 
     def tot_copy(i):
+        pos, to = 15 - (i >> 4), i & 15
         return pltpu.make_async_remote_copy(
-            src_ref=tot, dst_ref=back.at[my_owner],
-            send_sem=tot_send.at[i], recv_sem=tot_recv,
-            device_id=at(z, i // NY, c, i % NY), device_id_type=MESH,
+            src_ref=tot.at[seat(pos) >> 1], dst_ref=wts.at[z * 8 + my_owner],
+            send_sem=tot_send, recv_sem=tot_recv,
+            device_id=at(down(pos), to >> 2, c, to & 3), device_id_type=MESH,
         )
 
     @pl.when(handles)
@@ -382,49 +391,32 @@
                 total = jnp.sum(part, axis=0, keepdims=True) + jnp.sum(
                     colacc[q, :, h * 128 : h * 128 + 128], axis=0, keepdims=True
                 )
-                tot[q * 2 + h : q * 2 + h + 1, :] = total
+                tot[q * 2 + h] = total
 
         def send(i, _):
-            @pl.when(i == xy)
-            def _():
-                pltpu.make_async_copy(tot, back.at[my_owner], tot_recv).start()
-
-            @pl.when(i != xy)
+            tot_copy(i).start()
+            return 0
+
+        def send_here(i, _):
+            @pl.when(i - 240 != xy)
             def _():
                 tot_copy(i).start()
             return 0
 
-        lax.fori_loop(0, NX * NY, send, 0)
-
-    pltpu.make_async_copy(back, back, tot_recv).wait()
-    for j in range(8):
-        for k in range(8):
-            ret[k, j : j + 1, :] = back[j, k : k + 1, :]
-
-    def ret_copy(pos):
-        return pltpu.make_async_remote_copy(
-            src_ref=ret.at[pos // 2], dst_ref=wts.at[z],
-            send_sem=ret_send.at[pos], recv_sem=ret_recv,
-            device_id=at(down(pos), x, c, y), device_id_type=MESH,
-        )
-
-    def ret_start(pos, _):
-        ret_copy(pos).start()
-        return 0
-
-    lax.fori_loop(1, NZ, ret_start, 0)
-    wts[z] = ret[0]
-    pltpu.make_async_copy(
-        wts.at[pl.ds(0, NZ - 1)], wts.at[pl.ds(0, NZ - 1)], ret_recv
-    ).wait()
+        lax.fori_loop(0, 240, send, 0)
+        pltpu.make_async_copy(tot.at[0], wts.at[z * 8 + my_owner], tot_recv).start()
+        lax.fori_loop(240, 256, send_here, 0)
+
+    arrived = wts.at[pl.ds(0, NZ * 8)]
+    pltpu.make_async_copy(arrived, arrived, tot_recv).wait()
 
     code = meta[0]
-    table = wts[...].reshape(NZ * 8, 128).T
+    table = wts[: NZ * 8].reshape(NZ * 8, 128).T
     lines = jnp.where((code >> 5) == iota((NZ * 8, ROWS), 0), 1.0, 0.0)
     picked = jnp.dot(table, lines, precision=lax.Precision.HIGHEST, preferred_element_type=F32)
     ahead = ((code >> 8) - z) & (NZ - 1)
     pos = jnp.where(ahead == 0, 0, jnp.where(ahead <= 8, 2 * ahead - 1, 2 * (NZ - ahead)))
-    lane = (pos & 1) * 64 + xy * 4 + (code & 3)
+    lane = (seat(pos) & 1) * 64 + xy * 4 + (code & 3)
     total = jnp.sum(jnp.where(iota((128, ROWS), 0) == lane, picked, 0.0), axis=0, keepdims=True)
     out_ref[...] = 0.1 * jnp.log(total)
 
@@ -437,7 +429,6 @@
 
     def drain_z(pos, _):
         meta_copy(pos, 0).wait_send()
-        ret_copy(pos).wait_send()
         return 0
 
     lax.fori_loop(1, NZ, drain_z, 0)
@@ -460,13 +451,8 @@
 
         lax.fori_loop(0, 16, drain_sib, 0)
 
-        def drain_tot(i, _):
-            @pl.when(i != xy)
-            def _():
-                tot_copy(i).wait_send()
-            return 0
-
-        lax.fori_loop(0, NX * NY, drain_tot, 0)
+        sent = wts.at[pl.ds(0, 255)]
+        pltpu.make_async_copy(sent, sent, tot_send).wait()
 
 
 def per_device(embeddings, labels):
@@ -494,10 +480,8 @@
             vmem((1024, WIDE), BF16),
             vmem((1024, 128), F32),
             vmem((4, 8, 256), F32),
-            vmem((8, 128), F32),
-            vmem((8, 8, 128), F32),
-            vmem((8, 8, 128), F32),
-            vmem((NZ, 8, 128), F32),
+            vmem((8, 1, 128), F32),
+            vmem((2 * NZ * 8, 1, 128), F32),
             dma((2,)), pltpu.SemaphoreType.REGULAR((5,)),
             dma((2, 2, ROWS // PIECE)), dma((2, 2, ROWS // PIECE)),
             dma((5, 8)), dma((2,)), dma((2,)),
@@ -505,8 +489,7 @@
             dma((NZ,)),
             dma((8,)), dma,
             dma((4, 4)), dma((4, 4)),
-            dma((NX * NY,)), dma,
-            dma((NZ,)), dma,
+            dma, dma,
         ],
         compiler_params=pltpu.CompilerParams(
             collective_id=0, has_side_effects=True, vmem_limit_bytes=64 * 1024 * 1024

time: 71.3 us -> 68.6 us (0.962)
  Pallas kernels: 69.6 us -> 66.9 us
    pallas_call x1, Pallas kernels: 69.6 us -> 66.9 us  [per_device(): pl.pallas_call(kernel, out_shape=jax.ShapeDtypeStruct((1, ROWS), F32), in...]
where the time goes in v5:
time: 68.6 us; the launch traced here: 68 us
  Pallas kernels  66.9 us (98%)
  local copies, waits for them, and re-layouts  1.1 us (2%)
    pallas_call x1, Pallas kernels, per_device(): pl.pallas_call(kernel, out_shape=jax.ShapeDtypeStruct((1, ROWS), F32), in...  66.9 us

profile of v5, /device:TPU:1, one launch (start us, length us, event | category | flops | bytes accessed | tf_op | source)
XLA Modules:
  0.0 68.0 jit_solution(18380784917375007846)
XLA Ops:
  0.0 66.9 %soft_dedup.1 = f32[1,128]{1,0:T(1,128)} custom-call(bf16[128,768]{1,0:T(8,128)(2,1)} %emb_hbm.1, s32[1,128]{1,0:T(1,128)} %bitcast.2), custom_call_target="tpu_custom_call" | custom-call | tf_op jit(solution)/shard_map/soft_dedup/pallas_call | solution.py:461
  66.9 0.0 copy-start
  66.9 0.6 copy-done
  67.5 0.5 copy.4
Async XLA Ops:
  66.9 0.6 copy-start

commit v6 on v5

--- a/solution.py
+++ b/solution.py
@@ -225,6 +225,8 @@
         for j in range(4):
             opp_copy(way, j).start()
     send_near(0, unit)
+    send_near(1, raw.at[0, 0])
+    send_near(2, raw.at[1, 0])
 
     for way in range(2):
         for piece in range(pieces):
@@ -242,12 +244,10 @@
                 far_copy(way, g, j).start()
                 return 0
 
-            lax.fori_loop(0, 8, far_start, 0)
+            lax.fori_loop(0, 8, far_start, 0, unroll=True)
 
     for g in (4, 3, 2, 1, 0):
         send_far(g)
-    send_near(1, raw.at[0, 0])
-    send_near(2, raw.at[1, 0])
     send_near(3, raw.at[0, 1])
     send_near(4, raw.at[1, 1])
 
@@ -403,7 +403,7 @@
                 tot_copy(i).start()
             return 0
 
-        lax.fori_loop(0, 240, send, 0)
+        lax.fori_loop(0, 240, send, 0, unroll=8)
         pltpu.make_async_copy(tot.at[0], wts.at[z * 8 + my_owner], tot_recv).start()
         lax.fori_loop(240, 256, send_here, 0)
 

time: 68.6 us -> 66.9 us (0.975)
  Pallas kernels: 66.9 us -> 65.5 us
    pallas_call x1, Pallas kernels: 66.9 us -> 65.5 us  [per_device(): pl.pallas_call(kernel, out_shape=jax.ShapeDtypeStruct((1, ROWS), F32), in...]
where the time goes in v6:
time: 66.9 us; the launch traced here: 66.6 us
  Pallas kernels  65.5 us (98%)
  local copies, waits for them, and re-layouts  1.1 us (2%)
    pallas_call x1, Pallas kernels, per_device(): pl.pallas_call(kernel, out_shape=jax.ShapeDtypeStruct((1, ROWS), F32), in...  65.5 us

profile of v6, /device:TPU:1, one launch (start us, length us, event | category | flops | bytes accessed | tf_op | source)
XLA Modules:
  0.0 66.6 jit_solution(12971379601120122772)
XLA Ops:
  0.0 65.5 %soft_dedup.1 = f32[1,128]{1,0:T(1,128)} custom-call(bf16[128,768]{1,0:T(8,128)(2,1)} %emb_hbm.1, s32[1,128]{1,0:T(1,128)} %bitcast.2), custom_call_target="tpu_custom_call" | custom-call | tf_op jit(solution)/shard_map/soft_dedup/pallas_call | solution.py:461
  65.5 0.0 copy-start
  65.5 0.6 copy-done
  66.1 0.5 copy.4
Async XLA Ops:
  65.5 0.6 copy-start

commit v7 on v6

--- a/solution.py
+++ b/solution.py
@@ -238,16 +238,13 @@
 
         far_out[way] = to_blocks(meta[3 + way], first, 40, raw[way, 1])
 
-    def send_far(g):
-        for way in range(2):
-            def far_start(j, _, way=way):
+        for g in (4, 3, 2, 1, 0):
+            def far_start(j, _, g=g, way=way):
                 far_copy(way, g, j).start()
                 return 0
 
             lax.fori_loop(0, 8, far_start, 0, unroll=True)
 
-    for g in (4, 3, 2, 1, 0):
-        send_far(g)
     send_near(3, raw.at[0, 1])
     send_near(4, raw.at[1, 1])
 

time: 66.9 us -> 66.9 us (level)
  no operation moved by 1% of the time
where the time goes in v7:
time: 66.9 us; the launch traced here: 66.1 us
  Pallas kernels  64.9 us (97%)
  local copies, waits for them, and re-layouts  1.1 us (2%)
    pallas_call x1, Pallas kernels, per_device(): pl.pallas_call(kernel, out_shape=jax.ShapeDtypeStruct((1, ROWS), F32), in...  64.9 us

profile of v7, /device:TPU:1, one launch (start us, length us, event | category | flops | bytes accessed | tf_op | source)
XLA Modules:
  0.0 66.1 jit_solution(12336137689897052860)
XLA Ops:
  0.0 64.9 %soft_dedup.1 = f32[1,128]{1,0:T(1,128)} custom-call(bf16[128,768]{1,0:T(8,128)(2,1)} %emb_hbm.1, s32[1,128]{1,0:T(1,128)} %bitcast.2), custom_call_target="tpu_custom_call" | custom-call | tf_op jit(solution)/shard_map/soft_dedup/pallas_call | solution.py:458
  65.0 0.0 copy-start
  65.0 0.6 copy-done
  65.6 0.5 copy.4
Async XLA Ops:
  65.0 0.6 copy-start
